TPU v7x, 128 devices: a whole 4x4x4 slice. The times are simulated.
128 devices in a mesh: dp: 8 (over y, z_hi), seq: 16 (over z_lo, x, core).
Axes of the slice: x: 4, y: 4, z: 4 (z_hi: 2, z_lo: 2; z = z_hi * 2 + z_lo), core: 2. Of those that a mesh axis runs over, the one named last changes fastest.
Arguments:
- bases: int32 [4194304], P(('dp', 'seq')), parts along dimension 0, may hold values from 0 to 3
- stem_weight: bfloat16 [20, 768], replicated, may hold values from -2.5 to 2.5
- conv_weight: bfloat16 [5, 768, 1536], replicated, may hold values from -0.09375 to 0.09375
- row_proj: bfloat16 [1536, 128], replicated, may hold values from -0.15625 to 0.15625
- col_proj: bfloat16 [1536, 128], replicated, may hold values from -0.15625 to 0.15625
- pair_weight: bfloat16 [3, 3, 128, 128], replicated, may hold values from -0.1875 to 0.1875
- out_weight: bfloat16 [128], replicated, may hold values from -0.5 to 0.5
- targets: int32 [2048, 256], P(('dp', 'seq')), parts along dimension 0, may hold values from 0 to 15
Outputs:
- predicted: float32 [2048, 256], P(('dp', 'seq')), parts along dimension 0
- trunk_grad: float32 [2048, 1536], P(('dp', 'seq')), parts along dimension 0
There are 8 independent parts, one for each index of `dp`. A program takes and returns all parts, laid end to end along the dimension named above; an argument that names none is the same for every part. Nothing has to cross between parts.
All inputs are finite; a program needn't handle non-finite values.
Results may differ from a plain program's by a relative error of at most 0.015.
The roundings to bfloat16 on the way count: a program that leaves them out, or rounds other values in their place, can miss the bound.
Values may be sent and summed in bfloat16 or wider, within the bound.
A program may use at most 128 MiB of HBM per device.

v0:
```python
import math

import jax
import jax.numpy as jnp
from jax import lax
from jax.sharding import PartitionSpec as P

STEM_POOL = 128
TRUNK_POOL = 16
PAIR_DILATION = 8
NBINS = 16


def extended_2(array, sides, width):
    for axis, dim in sides:
        size, length = (lax.axis_size(axis), array.shape[dim])
        up = [(i, (i + 1) % size) for i in range(size - 1)]
        down = [(j, i) for i, j in up]
        last = lax.slice_in_dim(array, length - width, length, axis=dim)
        leading = lax.slice_in_dim(array, 0, width, axis=dim)
        before = lax.ppermute(last, axis, up)
        after = lax.ppermute(leading, axis, down)
        array = jnp.concatenate([before, array, after], axis=dim)
    return array


def gelu_slope(values):
    return jax.grad(lambda inner: jnp.sum(jax.nn.gelu(inner)))(values)


def stem_block(padded, first_row, stem_weight, block_len):
    window = lax.dynamic_slice_in_dim(padded, first_row, block_len + 4)
    base_codes = jnp.arange(1, 5, dtype=jnp.int32)
    columns = [
        window[offset : offset + block_len, None] == base_codes[None, :] for offset in range(5)
    ]
    onehot = jnp.concatenate(columns, axis=1).astype(jnp.bfloat16)
    activated = jax.nn.gelu(jnp.dot(onehot, stem_weight, preferred_element_type=jnp.float32))
    shaped = activated.reshape(block_len // STEM_POOL, STEM_POOL, activated.shape[1])
    return jnp.max(shaped, axis=1).astype(jnp.bfloat16)


def trunk_conv(extended, conv_weight, row_count):
    total_sum = jnp.zeros((row_count, conv_weight.shape[2]), jnp.float32)
    for offset in range(5):
        total_sum = total_sum + jnp.dot(
            extended[offset : offset + row_count],
            conv_weight[offset],
            preferred_element_type=jnp.float32,
        )
    activated = jax.nn.gelu(total_sum)
    shaped = activated.reshape(row_count // TRUNK_POOL, TRUNK_POOL, activated.shape[1])
    return jnp.max(shaped, axis=1)


def pair_taps(padded, weight, row_count, col_count, reverse):
    channels = weight.shape[3]
    total_sum = jnp.zeros((row_count * col_count, channels), jnp.float32)
    for kernel_row in range(3):
        for kernel_column in range(3):
            if reverse:
                row_begin = (2 - kernel_row) * PAIR_DILATION
                column_begin = (2 - kernel_column) * PAIR_DILATION
                matrix = weight[kernel_row, kernel_column].T
            else:
                row_begin = kernel_row * PAIR_DILATION
                column_begin = kernel_column * PAIR_DILATION
                matrix = weight[kernel_row, kernel_column]
            window = padded[
                row_begin : row_begin + row_count, column_begin : column_begin + col_count
            ]
            window = window.reshape(row_count * col_count, channels)
            total_sum = total_sum + jnp.dot(window, matrix, preferred_element_type=jnp.float32)
    return total_sum.reshape(row_count, col_count, channels)


def per_device(
    bases, stem_weight, conv_weight, row_proj, col_proj, pair_weight, out_weight, targets
):
    block_len = 4096
    local_bases = bases.shape[0]
    extended_bases = extended_2(bases + 1, (("seq", 0),), 2)
    starts = jnp.arange(local_bases // block_len) * block_len
    pooled1 = lax.map(
        lambda first_row: stem_block(extended_bases, first_row, stem_weight, block_len), starts
    )
    pooled1 = pooled1.reshape(local_bases // STEM_POOL, stem_weight.shape[1])
    extended = extended_2(pooled1, (("seq", 0),), 2)
    pooled2 = trunk_conv(extended, conv_weight, pooled1.shape[0])
    local_bins = pooled2.shape[0]
    bin_count = local_bins * lax.axis_size("seq")
    total_sum, squares = lax.psum(
        (jnp.sum(pooled2, axis=0), jnp.sum(pooled2 * pooled2, axis=0)), "seq"
    )
    channel_mean = total_sum / bin_count
    channel_var = squares / bin_count - channel_mean * channel_mean
    normed = ((pooled2 - channel_mean) * lax.rsqrt(channel_var + 1e-05)).astype(jnp.bfloat16)
    rows_emb = jnp.dot(normed, row_proj, preferred_element_type=jnp.float32).astype(jnp.bfloat16)
    cols_emb = jnp.dot(
        lax.all_gather(normed, "seq", axis=0, tiled=True),
        col_proj,
        preferred_element_type=jnp.float32,
    ).astype(jnp.bfloat16)
    cols_wide = cols_emb.astype(jnp.float32)[None, :, :]
    summed = rows_emb.astype(jnp.float32)[:, None, :] + cols_wide
    out_scale = out_weight.astype(jnp.float32)
    hidden_state = jax.nn.gelu(summed).astype(jnp.bfloat16)
    hidden_extended = extended_2(hidden_state, (("seq", 0),), PAIR_DILATION)
    hidden_padded = jnp.pad(hidden_extended, ((0, 0), (PAIR_DILATION, PAIR_DILATION), (0, 0)))
    conv_out = pair_taps(hidden_padded, pair_weight, local_bins, bin_count, False)
    predicted = jnp.sum(
        (hidden_state.astype(jnp.float32) + jax.nn.gelu(conv_out)) * out_scale, axis=-1
    )
    target_value = (targets.astype(jnp.float32) - (NBINS - 1) / 2.0) / (NBINS / 4.0)
    pred_grad = (predicted - target_value) / math.sqrt(bin_count)
    direct = pred_grad[:, :, None] * out_scale
    filter_gradient = (direct * gelu_slope(conv_out)).astype(jnp.bfloat16)
    gradient_extended = extended_2(filter_gradient, (("seq", 0),), PAIR_DILATION)
    gradient_padded = jnp.pad(gradient_extended, ((0, 0), (PAIR_DILATION, PAIR_DILATION), (0, 0)))
    hidden_grad = direct + pair_taps(gradient_padded, pair_weight, local_bins, bin_count, True)
    sum_grad = hidden_grad * gelu_slope(summed)
    row_grad = jnp.sum(sum_grad, axis=1)
    col_part = jnp.sum(sum_grad, axis=0)
    row_term = jnp.dot(
        row_grad,
        row_proj.astype(jnp.float32).T,
        precision=lax.Precision.HIGHEST,
        preferred_element_type=jnp.float32,
    )
    col_matrix = col_proj.astype(jnp.float32).T
    col_term = lax.psum_scatter(
        jnp.dot(
            col_part,
            col_matrix,
            precision=lax.Precision.HIGHEST,
            preferred_element_type=jnp.float32,
        ).astype(jnp.bfloat16),
        "seq",
        scatter_dimension=0,
        tiled=True,
    ).astype(jnp.float32)
    return (predicted, row_term + col_term)


def solution(mesh):
    in_specs = (P(("dp", "seq")), P(), P(), P(), P(), P(), P(), P(("dp", "seq"), None))
    out_specs = (P(("dp", "seq"), None), P(("dp", "seq"), None))
    return jax.shard_map(
        per_device, mesh=mesh, in_specs=in_specs, out_specs=out_specs, check_vma=False
    )
```

profile of v0, /device:TPU:1, one launch (start us, length us, event | category | flops | bytes accessed | tf_op | source)
XLA Modules:
  0.0 302.0 jit_solution(5925924763599664409)
XLA Ops:
  7.2 1.0 broadcast_add_fusion.1
  8.3 4.5 %collective-permute-start = (s32[2]{0:T(128)S(1)}, s32[2]{0:T(128)S(1)}, u32[]{:S(2)}, u32[]{:S(2)}) collective-permute-start(s32[2]{0:T(128)S(1)} %get-tuple-element.81), channel_id=1, source_target_pairs={{0,1},{1,2},{2,3},{3,4},{4,5},{5,6},{6,7},{7,8},{8,9},{9,10},{10,1... | collective-permute-start | bytes 32 | tf_op jit(solution)/shard_map/ppermute | solution.py:21
  12.8 1.9 collective-permute-start.1
  14.7 2.9 collective-permute-done.1
  17.8 69.2 %while.10 = (s32[]{:T(128)}, bf16[8,32,768]{2,1,0:T(8,128)(2,1)S(1)}, s32[8]{0:T(128)S(1)}, s32[32772]{0:T(1024)S(1)}, bf16[20,768]{1,0:T(8,128)(2,1)}, /*index=...) while((s32[]{:T(128)}, bf16[8,32,768]{2,1,0:T(8,128)(2,1)S(1)}, s32[8]{0:T(128)S(1)}, ...), condition=%wide.region_2.3_spmd, body=%wide.region_0.2_spmd.sunk | while | flops 154198032 | bytes 751883 | solution.py:84
  17.8 0.6 dynamic_slice.8
  20.8 5.6 %bitcast_reduce_fusion.3 = bf16[32,768]{1,0:T(8,128)(2,1)S(1)} fusion(pred[4096,20]{0,1:T(8,128)(4,1)S(1)} %concatenate.43, bf16[20,768]{1,0:T(8,128)(2,1)} %get-tuple-element.165), kind=kOutput, calls=%fused_computation.8.clone.1 | convolution fusion | flops 154116096 | bytes 161792 | tf_op jit(solution)/shard_map/while/body/eval_jaxpr/dot_general | solution.py:38
  26.4 0.6 dynamic_slice.8
  29.4 5.6 %bitcast_reduce_fusion.3 = bf16[32,768]{1,0:T(8,128)(2,1)S(1)} fusion(pred[4096,20]{0,1:T(8,128)(4,1)S(1)} %concatenate.43, bf16[20,768]{1,0:T(8,128)(2,1)} %get-tuple-element.165), kind=kOutput, calls=%fused_computation.8.clone.1 | convolution fusion | flops 154116096 | bytes 161792 | tf_op jit(solution)/shard_map/while/body/eval_jaxpr/dot_general | solution.py:38
  35.1 0.6 dynamic_slice.8
  38.0 5.6 %bitcast_reduce_fusion.3 = bf16[32,768]{1,0:T(8,128)(2,1)S(1)} fusion(pred[4096,20]{0,1:T(8,128)(4,1)S(1)} %concatenate.43, bf16[20,768]{1,0:T(8,128)(2,1)} %get-tuple-element.165), kind=kOutput, calls=%fused_computation.8.clone.1 | convolution fusion | flops 154116096 | bytes 161792 | tf_op jit(solution)/shard_map/while/body/eval_jaxpr/dot_general | solution.py:38
  43.7 0.6 dynamic_slice.8
  46.7 5.6 %bitcast_reduce_fusion.3 = bf16[32,768]{1,0:T(8,128)(2,1)S(1)} fusion(pred[4096,20]{0,1:T(8,128)(4,1)S(1)} %concatenate.43, bf16[20,768]{1,0:T(8,128)(2,1)} %get-tuple-element.165), kind=kOutput, calls=%fused_computation.8.clone.1 | convolution fusion | flops 154116096 | bytes 161792 | tf_op jit(solution)/shard_map/while/body/eval_jaxpr/dot_general | solution.py:38
  52.3 0.6 dynamic_slice.8
  55.3 5.6 %bitcast_reduce_fusion.3 = bf16[32,768]{1,0:T(8,128)(2,1)S(1)} fusion(pred[4096,20]{0,1:T(8,128)(4,1)S(1)} %concatenate.43, bf16[20,768]{1,0:T(8,128)(2,1)} %get-tuple-element.165), kind=kOutput, calls=%fused_computation.8.clone.1 | convolution fusion | flops 154116096 | bytes 161792 | tf_op jit(solution)/shard_map/while/body/eval_jaxpr/dot_general | solution.py:38
  61.0 0.6 dynamic_slice.8
  64.0 5.6 %bitcast_reduce_fusion.3 = bf16[32,768]{1,0:T(8,128)(2,1)S(1)} fusion(pred[4096,20]{0,1:T(8,128)(4,1)S(1)} %concatenate.43, bf16[20,768]{1,0:T(8,128)(2,1)} %get-tuple-element.165), kind=kOutput, calls=%fused_computation.8.clone.1 | convolution fusion | flops 154116096 | bytes 161792 | tf_op jit(solution)/shard_map/while/body/eval_jaxpr/dot_general | solution.py:38
  69.6 0.6 dynamic_slice.8
  72.6 5.6 %bitcast_reduce_fusion.3 = bf16[32,768]{1,0:T(8,128)(2,1)S(1)} fusion(pred[4096,20]{0,1:T(8,128)(4,1)S(1)} %concatenate.43, bf16[20,768]{1,0:T(8,128)(2,1)} %get-tuple-element.165), kind=kOutput, calls=%fused_computation.8.clone.1 | convolution fusion | flops 154116096 | bytes 161792 | tf_op jit(solution)/shard_map/while/body/eval_jaxpr/dot_general | solution.py:38
  78.3 0.6 dynamic_slice.8
  81.3 5.6 %bitcast_reduce_fusion.3 = bf16[32,768]{1,0:T(8,128)(2,1)S(1)} fusion(pred[4096,20]{0,1:T(8,128)(4,1)S(1)} %concatenate.43, bf16[20,768]{1,0:T(8,128)(2,1)} %get-tuple-element.165), kind=kOutput, calls=%fused_computation.8.clone.1 | convolution fusion | flops 154116096 | bytes 161792 | tf_op jit(solution)/shard_map/while/body/eval_jaxpr/dot_general | solution.py:38
  86.9 2.0 collective-permute-start.2
  88.9 2.4 fusion.16
  91.4 2.3 collective-permute-start.3
  93.7 2.4 fusion.18
  96.3 2.4 fusion.13
  98.7 2.5 fusion.12
  101.2 3.0 bitcast_reduce_fusion.1
  104.2 50.9 %all-reduce.2 = (f32[1536]{0:T(1024)S(1)}, f32[1536]{0:T(1024)S(1)}) all-reduce(f32[1536]{0:T(1024)S(1)} %get-tuple-element.33, f32[1536]{0:T(1024)S(1)} %get-tuple-element.32), channel_id=1, replica_groups=mesh['dp'=8,'seq'=16] {'seq'}, use_global_device_ids=true, to_apply=%region_7.8 | all-reduce | flops 3072 | bytes 24576 | tf_op jit(solution)/shard_map/psum | solution.py:92
  155.2 25.1 %all_gather.3 = bf16[256,1536]{1,0:T(8,128)(2,1)S(1)} all-gather(bf16[16,1536]{1,0:T(8,128)(2,1)S(1)} %multiply_convert_fusion), channel_id=1, replica_groups=mesh['dp'=8,'seq'=16] {'seq'}, dimensions={0}, use_global_device_ids=true | all-gather | bytes 835584 | tf_op jit(solution)/shard_map/all_gather | solution.py:100
  180.9 0.8 broadcast_add_fusion
  181.7 3.1 %collective-permute-start.4 = (bf16[8,256,128]{2,1,0:T(8,128)(2,1)S(1)}, bf16[8,256,128]{2,1,0:T(8,128)(2,1)S(1)}, u32[]{:S(2)}, u32[]{:S(2)}) collective-permute-start(bf16[8,256,128]{2,1,0:T(8,128)(2,1)S(1)} %get-tuple-element.74), channel_id=1, source_target_pairs={{0,1},{1,2},{2,3},{3,4},{4,5},{5,6},{6,7},{7,8},{8,9},{9,10},{10,1... | collective-permute-start | bytes 1572872 | tf_op jit(solution)/shard_map/ppermute | solution.py:21
  184.9 2.1 collective-permute-start.5
  187.0 4.0 %collective-permute-done.4 = bf16[8,256,128]{2,1,0:T(8,128)(2,1)S(1)} collective-permute-done((bf16[8,256,128]{2,1,0:T(8,128)(2,1)S(1)}, bf16[8,256,128]{2,1,0:T(8,128)(2,1)S(1)}, u32[]{:S(2)}, u32[]{:S(2)}) %collective-permute-start.4) | collective-permute-done | bytes 524320 | tf_op jit(solution)/shard_map/ppermute | solution.py:21
  191.0 4.4 %collective-permute-done.5 = bf16[8,256,128]{2,1,0:T(8,128)(2,1)S(1)} collective-permute-done((bf16[8,256,128]{2,1,0:T(8,128)(2,1)S(1)}, bf16[8,256,128]{2,1,0:T(8,128)(2,1)S(1)}, u32[]{:S(2)}, u32[]{:S(2)}) %collective-permute-start.5) | collective-permute-done | bytes 524320 | tf_op jit(solution)/shard_map/ppermute | solution.py:22
  195.4 0.9 select_maximum_fusion.2
  196.3 1.1 fusion.141
  197.8 0.4 fusion.89
  198.4 0.4 convolution_add_fusion.13
  198.9 0.4 convolution_add_fusion.12
  199.3 0.4 convolution_add_fusion.11
  199.7 0.4 convolution_add_fusion.10
  200.1 0.4 convolution_add_fusion.9
  201.0 1.8 multiply_reduce_fusion
  202.9 1.5 fusion.38
  204.5 1.9 collective-permute-start.6
  206.4 2.7 collective-permute-start.7
  209.1 3.4 %collective-permute-done.6 = bf16[8,256,128]{2,1,0:T(8,128)(2,1)S(1)} collective-permute-done((bf16[8,256,128]{2,1,0:T(8,128)(2,1)S(1)}, bf16[8,256,128]{2,1,0:T(8,128)(2,1)S(1)}, u32[]{:S(2)}, u32[]{:S(2)}) %collective-permute-start.6) | collective-permute-done | bytes 524320 | tf_op jit(solution)/shard_map/ppermute | solution.py:21
  212.5 4.4 %collective-permute-done.7 = bf16[8,256,128]{2,1,0:T(8,128)(2,1)S(1)} collective-permute-done((bf16[8,256,128]{2,1,0:T(8,128)(2,1)S(1)}, bf16[8,256,128]{2,1,0:T(8,128)(2,1)S(1)}, u32[]{:S(2)}, u32[]{:S(2)}) %collective-permute-start.7) | collective-permute-done | bytes 524320 | tf_op jit(solution)/shard_map/ppermute | solution.py:22
  216.9 0.9 select_maximum_fusion
  217.8 1.1 fusion.140
  218.9 0.4 fusion.105
  219.4 0.4 fusion.87
  220.0 0.4 convolution_add_fusion.6
  220.4 0.4 convolution_add_fusion.5
  220.9 0.4 convolution_add_fusion.4
  221.3 1.6 convolution_add_fusion.3
  222.9 0.4 convolution_add_fusion.2
  223.4 0.4 convolution_add_fusion.1
  223.8 0.5 fusion.7
  224.3 1.8 fusion.137
  226.1 1.7 convolution_convert_fusion
  227.8 65.5 %reduce-scatter.2.cloned.1.call-done = bf16[16,1536]{1,0:T(8,128)(2,1)} async-done(((bf16[256,1536]{1,0:T(8,128)(2,1)}), bf16[16,1536]{1,0:T(8,128)(2,1)}) %reduce-scatter.2.cloned.1.call-update) | async-done | bytes 49168 | tf_op jit(solution)/shard_map/reduce_scatter | solution.py:131
  293.3 1.9 convolution_add_fusion.16
  (77 shorter events, 6.1 us)
Async XLA Ops:
  7.2 173.3 %copy-start = (bf16[1536,128]{1,0:T(8,128)(2,1)S(1)}, bf16[1536,128]{1,0:T(8,128)(2,1)}, u32[]{:S(2)}) copy-start(bf16[1536,128]{1,0:T(8,128)(2,1)} %param.14) | copy-start | bytes 1179652
  7.2 286.1 %reduce-scatter.2.cloned.1.call-start = ((), (), s32[]{:S(2)}) async-start(), calls=%async_computation.1 | async-start | bytes 835584 | tf_op jit(solution)/shard_map/reduce_scatter | solution.py:131
  8.3 6.5 %collective-permute-start = (s32[2]{0:T(128)S(1)}, s32[2]{0:T(128)S(1)}, u32[]{:S(2)}, u32[]{:S(2)}) collective-permute-start(s32[2]{0:T(128)S(1)} %get-tuple-element.81), channel_id=1, source_target_pairs={{0,1},{1,2},{2,3},{3,4},{4,5},{5,6},{6,7},{7,8},{8,9},{9,10},{10,1... | collective-permute-start | bytes 32 | tf_op jit(solution)/shard_map/ppermute | solution.py:21
  12.8 4.9 %collective-permute-start.1 = (s32[2]{0:T(128)S(1)}, s32[2]{0:T(128)S(1)}, u32[]{:S(2)}, u32[]{:S(2)}) collective-permute-start(s32[2]{0:T(128)S(1)} %get-tuple-element.80), channel_id=1, source_target_pairs={{1,0},{2,1},{3,2},{4,3},{5,4},{6,5},{7,6},{8,7},{9,8},{10,9},{11,1... | collective-permute-start | bytes 32 | tf_op jit(solution)/shard_map/ppermute | solution.py:22
  86.9 6.8 %collective-permute-start.2 = (bf16[2,768]{1,0:T(2,128)(2,1)S(1)}, bf16[2,768]{1,0:T(2,128)(2,1)S(1)}, u32[]{:S(2)}, u32[]{:S(2)}) collective-permute-start(bf16[2,768]{1,0:T(2,128)(2,1)S(1)} %get-tuple-element.76), channel_id=1, source_target_pairs={{0,1},{1,2},{2,3},{3,4},{4,5},{5,6},{6,7},{7,8},{8,9},{9,10},{10,1... | collective-permute-start | bytes 9224 | tf_op jit(solution)/shard_map/ppermute | solution.py:21
  91.4 4.9 %collective-permute-start.3 = (bf16[2,768]{1,0:T(2,128)(2,1)S(1)}, bf16[2,768]{1,0:T(2,128)(2,1)S(1)}, u32[]{:S(2)}, u32[]{:S(2)}) collective-permute-start(bf16[2,768]{1,0:T(2,128)(2,1)S(1)} %get-tuple-element.77), channel_id=1, source_target_pairs={{1,0},{2,1},{3,2},{4,3},{5,4},{6,5},{7,6},{8,7},{9,8},{10,9},{11,1... | collective-permute-start | bytes 9224 | tf_op jit(solution)/shard_map/ppermute | solution.py:22
  101.2 79.1 %copy-start.1 = (bf16[1536,128]{1,0:T(8,128)(2,1)S(1)}, bf16[1536,128]{1,0:T(8,128)(2,1)}, u32[]{:S(2)}) copy-start(bf16[1536,128]{1,0:T(8,128)(2,1)} %param.13) | copy-start | bytes 1179652
  180.9 6.1 %copy-start.5 = (bf16[128]{0:T(256)(128)(2,1)S(1)}, bf16[128]{0:T(256)(128)(2,1)}, u32[]{:S(2)}) copy-start(bf16[128]{0:T(256)(128)(2,1)} %param.16) | copy-start | bytes 772
  181.7 9.3 %collective-permute-start.4 = (bf16[8,256,128]{2,1,0:T(8,128)(2,1)S(1)}, bf16[8,256,128]{2,1,0:T(8,128)(2,1)S(1)}, u32[]{:S(2)}, u32[]{:S(2)}) collective-permute-start(bf16[8,256,128]{2,1,0:T(8,128)(2,1)S(1)} %get-tuple-element.74), channel_id=1, source_target_pairs={{0,1},{1,2},{2,3},{3,4},{4,5},{5,6},{6,7},{7,8},{8,9},{9,10},{10,1... | collective-permute-start | bytes 1572872 | tf_op jit(solution)/shard_map/ppermute | solution.py:21
  184.9 10.5 %collective-permute-start.5 = (bf16[8,256,128]{2,1,0:T(8,128)(2,1)S(1)}, bf16[8,256,128]{2,1,0:T(8,128)(2,1)S(1)}, u32[]{:S(2)}, u32[]{:S(2)}) collective-permute-start(bf16[8,256,128]{2,1,0:T(8,128)(2,1)S(1)} %get-tuple-element.75), channel_id=1, source_target_pairs={{1,0},{2,1},{3,2},{4,3},{5,4},{6,5},{7,6},{8,7},{9,8},{10,9},{11,1... | collective-permute-start | bytes 1572872 | tf_op jit(solution)/shard_map/ppermute | solution.py:22
  196.3 1.1 copy-start.2
  201.0 1.9 copy-start.4
  202.8 1.6 copy-start.3
  204.5 8.0 %collective-permute-start.6 = (bf16[8,256,128]{2,1,0:T(8,128)(2,1)S(1)}, bf16[8,256,128]{2,1,0:T(8,128)(2,1)S(1)}, u32[]{:S(2)}, u32[]{:S(2)}) collective-permute-start(bf16[8,256,128]{2,1,0:T(8,128)(2,1)S(1)} %get-tuple-element.70), channel_id=1, source_target_pairs={{0,1},{1,2},{2,3},{3,4},{4,5},{5,6},{6,7},{7,8},{8,9},{9,10},{10,1... | collective-permute-start | bytes 1572872 | tf_op jit(solution)/shard_map/ppermute | solution.py:21
  206.4 10.5 %collective-permute-start.7 = (bf16[8,256,128]{2,1,0:T(8,128)(2,1)S(1)}, bf16[8,256,128]{2,1,0:T(8,128)(2,1)S(1)}, u32[]{:S(2)}, u32[]{:S(2)}) collective-permute-start(bf16[8,256,128]{2,1,0:T(8,128)(2,1)S(1)} %get-tuple-element.71), channel_id=1, source_target_pairs={{1,0},{2,1},{3,2},{4,3},{5,4},{6,5},{7,6},{8,7},{9,8},{10,9},{11,1... | collective-permute-start | bytes 1572872 | tf_op jit(solution)/shard_map/ppermute | solution.py:22
Sparse Core Ops, SparseCore 0:
  227.9 65.3 reduce-scatter.1
where the time goes:
time: 306 us; the launch traced here: 302 us
  waiting for transfers between devices  84.7 us (28%)
  blocking collectives  76 us (25%)
  matrix products  72 us (24%)
  starting transfers between devices  20.6 us (7%)
  loops' own time  15.9 us (5%)
  between operations  14.5 us (5%)
  local copies, waits for them, and re-layouts  9.61 us (3%)
  other arithmetic  8.6 us (3%)
    reduce_scatter x1, waiting for transfers between devices, per_device(): lax.psum_scatter(jnp.dot(col_part, col_matrix, precision=lax.Precision.HI...  65.5 us
    psum x1, blocking collectives, per_device(): lax.psum((jnp.sum(pooled2, axis=0), jnp.sum(pooled2 * pooled2, axis=0)),...  50.9 us
    dot_general x8, matrix products, stem_block(): jnp.dot(onehot, stem_weight, preferred_element_type=jnp.float32)  44.9 us
    all_gather x1, blocking collectives, per_device(): lax.all_gather(normed, 'seq', axis=0, tiled=True)  25.1 us
    another operation x1, loops' own time, per_device(): lax.map(lambda first_row: stem_block(extended_bases, first_row, stem_weig...  15.9 us
    dot_general x5, matrix products, trunk_conv(): jnp.dot(extended[offset:offset + row_count], conv_weight[offset], preferr...  12.8 us
    ppermute x4, waiting for transfers between devices, extended_2(): after = lax.ppermute(leading, axis, down)  11.8 us
    ppermute x4, starting transfers between devices, extended_2(): before = lax.ppermute(last, axis, up)  11.5 us
  transfers between devices with their start and end apart: 9, of which 7 were waited for; matrix products, arithmetic and copies ran while one was open for 2% of the time, Pallas kernels for 0%

commit v1 on v0

v1 whole, which is shorter than its diff:
```python
import functools
import math

import jax
import jax.numpy as jnp
from jax import lax
from jax.experimental import pallas as pl
from jax.experimental.pallas import tpu as pltpu
from jax.sharding import PartitionSpec as P

MESH = pl.DeviceIdType.MESH
F32 = jnp.float32
BF16 = jnp.bfloat16

N_SEQ = 16
STEM_CH = 768
TRUNK_CH = 1536
CH = 128
POOL = 128
ROWS = 256
BINS = 256
LOCAL = 16
GROUP = 24
TILES = TRUNK_CH // 256
C0 = math.sqrt(2.0 / math.pi)


def gelu(x):
    half = 0.5 * x
    return half + half * jnp.tanh(x * (C0 + (C0 * 0.044715) * (x * x)))


def gelu_and_slope(x):
    square = x * x
    t = jnp.tanh(x * (C0 + (C0 * 0.044715) * square))
    half = 0.5 * x
    slope = 0.5 + 0.5 * t + half * (1.0 - t * t) * (C0 + (3.0 * C0 * 0.044715) * square)
    return half + half * t, slope


def fused(
    bases_ref,
    stem_ref,
    conv_ref,
    row_proj_ref,
    col_proj_ref,
    pair_ref,
    out_w_ref,
    targets_ref,
    pred_ref,
    grad_ref,
    halo,
    ext,
    codes,
    stem_w,
    pooled1,
    lhs,
    conv_w,
    pooled2,
    stat_out,
    stat_in,
    emb_out,
    emb_in,
    tgt_out,
    tgt_in,
    tgt_rows,
    tgt_t,
    fwd_w,
    bwd_w,
    rows_scr,
    hid,
    slope_scr,
    direct_scr,
    cgrad,
    pred_t,
    pred_out_s,
    pred_in,
    rowsum,
    part_out,
    part_in,
    conv_sems,
    halo_send,
    halo_recv,
    send_sems,
    recv_sems,
):
    me = lax.axis_index("seq")
    rho = me // 2
    half = me % 2
    first = me == 0
    last = me == N_SEQ - 1

    for q in range(TILES):
        pltpu.make_async_copy(
            conv_ref.at[:, pl.ds(256 * q, 256)], conv_w.at[q], conv_sems.at[q]
        ).start()

    barrier = pltpu.get_barrier_semaphore()

    def greet(k, carry):
        peer = lax.rem(me + k, N_SEQ)
        pl.semaphore_signal(barrier, inc=1, device_id={"seq": peer}, device_id_type=MESH)
        return carry

    lax.fori_loop(1, N_SEQ, greet, 0)

    ext[...] = jnp.zeros_like(ext)
    ext[8 : 8 + ROWS, :] = bases_ref[...] + 1
    for r in range(8):
        tgt_out[r, 0:1, :] = targets_ref[r : r + 1, :]
        tgt_out[r, 1:2, :] = targets_ref[r + 8 : r + 9, :]
    stem_w[...] = jnp.zeros_like(stem_w)
    stem_w[0:20, :] = stem_ref[...].astype(F32)

    pl.semaphore_wait(barrier, N_SEQ - 1)

    def send_all(index, source_of, landing):
        def one(k, carry):
            peer = lax.rem(me + k, N_SEQ)
            pltpu.make_async_remote_copy(
                src_ref=source_of(peer),
                dst_ref=landing.at[me],
                send_sem=send_sems.at[index],
                recv_sem=recv_sems.at[index],
                device_id={"seq": peer},
                device_id_type=MESH,
            ).start()
            return carry

        lax.fori_loop(1, N_SEQ, one, 0)

    def wait_recv(index, landing):
        blocks = landing.at[pl.ds(0, N_SEQ - 1)]
        pltpu.make_async_copy(blocks, blocks, recv_sems.at[index]).wait()

    def wait_send(index, landing):
        blocks = landing.at[pl.ds(0, N_SEQ - 1)]
        pltpu.make_async_copy(blocks, blocks, send_sems.at[index]).wait()

    up = pltpu.make_async_remote_copy(
        src_ref=bases_ref.at[pl.ds(ROWS - 8, 8)],
        dst_ref=halo.at[0],
        send_sem=halo_send.at[0],
        recv_sem=halo_recv.at[0],
        device_id={"seq": lax.rem(me + 1, N_SEQ)},
        device_id_type=MESH,
    )
    down = pltpu.make_async_remote_copy(
        src_ref=bases_ref.at[pl.ds(0, 8)],
        dst_ref=halo.at[1],
        send_sem=halo_send.at[1],
        recv_sem=halo_recv.at[1],
        device_id={"seq": lax.rem(me + N_SEQ - 1, N_SEQ)},
        device_id_type=MESH,
    )
    up.start()
    down.start()
    send_all(0, lambda peer: tgt_out.at[peer // 2], tgt_in)
    tgt_in[pl.ds(me, 1)] = tgt_out[pl.ds(rho, 1)]

    lane = lax.broadcasted_iota(jnp.int32, (1, POOL), 1)

    def code_rows(start, count):
        total = ext[start : start + count, :] << 6
        here = ext[start : start + count, :]
        above = ext[start - 1 : start - 1 + count, :]
        below = ext[start + 1 : start + 1 + count, :]
        for shift in (1, 2):
            before = jnp.where(
                lane >= shift, pltpu.roll(here, shift, 1), pltpu.roll(above, shift, 1)
            )
            after = jnp.where(
                lane < POOL - shift,
                pltpu.roll(here, POOL - shift, 1),
                pltpu.roll(below, POOL - shift, 1),
            )
            total = total + (before << (3 * (2 - shift))) + (after << (3 * (2 + shift)))
        return total

    codes[0:240, :] = code_rows(16, 240)

    sub = lax.broadcasted_iota(jnp.int32, (8, POOL), 0)
    base_code = (sub & 3) + 1
    tap_shift = (sub >> 2) * 3
    zero_rows = jnp.zeros((8, POOL), F32)

    def stem_step(start):
        pieces = []
        for r in range(GROUP):
            code = jnp.broadcast_to(codes[pl.ds(start + r, 1), :], (8, POOL))
            taps = [
                jnp.where(((code >> (tap_shift + 6 * k)) & 7) == base_code, 1.0, 0.0).astype(F32)
                for k in range(3)
            ]
            pieces.append(jnp.concatenate(taps + [zero_rows], axis=0).astype(BF16))
        onehot = jnp.concatenate(pieces, axis=1)
        parts = []
        for n in range(STEM_CH // 256):
            stem = lax.dot_general(
                onehot,
                stem_w[:, 256 * n : 256 * n + 256].astype(BF16),
                (((0,), (0,)), ((), ())),
                preferred_element_type=F32,
            ).reshape(GROUP, POOL, 256)
            parts.append(
                jnp.maximum(gelu(jnp.max(stem, axis=1)), gelu(jnp.min(stem, axis=1)))
            )
        return jnp.concatenate(parts, axis=1).astype(BF16).astype(F32)

    def stem_body(g, carry):
        start = pl.multiple_of(g * GROUP, 8)
        pooled1[pl.ds(pl.multiple_of(16 + g * GROUP, 8), GROUP), :] = stem_step(start)
        return carry

    lax.fori_loop(0, 10, stem_body, 0)

    up.wait()
    down.wait()
    ext[0:8, :] = jnp.where(first, 0, halo[0] + 1)
    ext[8 + ROWS : 16 + ROWS, :] = jnp.where(last, 0, halo[1] + 1)
    codes[240:250, :] = code_rows(6, 10)
    codes[250:260, :] = code_rows(256, 10)
    codes[260:264, :] = jnp.zeros((4, POOL), jnp.int32)
    edge = stem_step(240)
    pooled1[6:16, :] = edge[0:10]
    pooled1[256:266, :] = edge[10:20]
    pooled1[6:8, :] = jnp.where(first, 0.0, edge[0:2])
    pooled1[264:266, :] = jnp.where(last, 0.0, edge[18:20])

    for k in range(5):
        lhs[:, STEM_CH * k : STEM_CH * k + STEM_CH] = pooled1[6 + k : 6 + k + ROWS, :].astype(BF16)

    for q in range(TILES):
        pltpu.make_async_copy(
            conv_ref.at[:, pl.ds(256 * q, 256)], conv_w.at[q], conv_sems.at[q]
        ).wait()

    def trunk_body(q, carry):
        trunk = jnp.dot(lhs[...], conv_w[q], preferred_element_type=F32)
        trunk = trunk.reshape(LOCAL, 16, 256)
        pooled2[q] = jnp.maximum(
            gelu(jnp.max(trunk, axis=1)), gelu(jnp.min(trunk, axis=1))
        )
        return carry

    lax.fori_loop(0, TILES, trunk_body, 0)

    sums = []
    squares = []
    for q in range(TILES):
        block = pooled2[q]
        sums.append(jnp.sum(block, axis=0, keepdims=True))
        squares.append(jnp.sum(block * block, axis=0, keepdims=True))
    for a in range(3):
        stat_out[a : a + 1, :] = jnp.concatenate(sums[2 * a : 2 * a + 2], axis=1)
        stat_out[4 + a : 5 + a, :] = jnp.concatenate(squares[2 * a : 2 * a + 2], axis=1)
    stat_out[3:4, :] = jnp.zeros((1, 512), F32)
    stat_out[7:8, :] = jnp.zeros((1, 512), F32)
    send_all(1, lambda peer: stat_out, stat_in)
    stat_in[pl.ds(me, 1)] = stat_out[...][None]

    zero_block = jnp.zeros((CH, CH), BF16)
    for a in range(4):
        for b in range(3):
            at = (3 * a + b) * CH
            near = pair_ref[(3 * a + b) * CH : (3 * a + b + 1) * CH, :] if a < 3 else zero_block
            far = (
                pair_ref[(3 * (a - 1) + b) * CH : (3 * (a - 1) + b + 1) * CH, :]
                if a > 0
                else zero_block
            )
            fwd_w[at : at + CH, :] = jnp.concatenate([near, far], axis=1)
            near = (
                pair_ref[(3 * (2 - a) + 2 - b) * CH : (3 * (2 - a) + 3 - b) * CH, :].T
                if a < 3
                else zero_block
            )
            far = (
                pair_ref[(3 * (3 - a) + 2 - b) * CH : (3 * (3 - a) + 3 - b) * CH, :].T
                if a > 0
                else zero_block
            )
            bwd_w[at : at + CH, :] = jnp.concatenate([near, far], axis=1)

    wait_recv(0, tgt_in)
    tgt_rows[...] = jnp.zeros_like(tgt_rows)
    for d in range(N_SEQ):
        tgt_rows[2 * d : 2 * d + 2, :] = tgt_in[d].astype(F32)
    tgt_t[...] = tgt_rows[...].T

    def chain_order(load):
        pieces = []
        for q in range(8):
            for s in range(4):
                pieces.append(load(q + 8 * s))
        return jnp.concatenate(pieces, axis=0)

    target = chain_order(lambda m: tgt_t[pl.ds(8 * m + 4 * half, 4), :])
    target = (target - 7.5) * 0.25

    zero_tile = jnp.zeros((16, CH), BF16)
    zero_row = jnp.zeros((160, CH), BF16)
    hid[0] = zero_row
    hid[33] = zero_row
    cgrad[0] = zero_row
    cgrad[33] = zero_row

    wait_recv(1, stat_in)
    total = jnp.sum(stat_in[...], axis=0)
    mean = total[0:4] / BINS
    var = total[4:8] / BINS - mean * mean
    scale = lax.rsqrt(var + 1e-05)
    normed = []
    for q in range(TILES):
        a, c = q // 2, 256 * (q % 2)
        normed.append(
            ((pooled2[q] - mean[a : a + 1, c : c + 256]) * scale[a : a + 1, c : c + 256]).astype(
                BF16
            )
        )
    normed = jnp.concatenate(normed, axis=1)
    proj = jnp.concatenate([row_proj_ref[...], col_proj_ref[...]], axis=1)
    emb = jnp.dot(normed, proj, preferred_element_type=F32).astype(BF16).astype(F32)
    rows_emb = emb[:, 0:CH]
    cols_emb = emb[:, CH : 2 * CH]
    for h in range(2):
        block = jnp.concatenate([cols_emb[4 * h : 4 * h + 4], cols_emb[8 + 4 * h : 12 + 4 * h]], 0)
        for r in range(8):
            emb_out[2 * r + h, 0:8, :] = block
            emb_out[2 * r + h, 8:9, :] = rows_emb[r : r + 1]
            emb_out[2 * r + h, 9:10, :] = rows_emb[r + 8 : r + 9]
            emb_out[2 * r + h, 10:16, :] = jnp.zeros((6, CH), F32)
    send_all(2, lambda peer: emb_out.at[peer], emb_in)
    emb_in[pl.ds(me, 1)] = emb_out[pl.ds(me, 1)]
    wait_recv(2, emb_in)

    for d in range(N_SEQ):
        rows_scr[2 * d : 2 * d + 2, :] = emb_in[d, 8:10, :]
    cols = chain_order(lambda m: emb_in[m // 2, 4 * (m % 2) : 4 * (m % 2) + 4, :])
    zero_four = jnp.zeros((4, CH), F32)

    def put_row(ref, index, values):
        ref[index, 16:144, :] = values.astype(BF16)
        ref[index, 0:16, :] = jnp.concatenate([zero_four, values[112:124]], axis=0).astype(BF16)
        ref[index, 144:160, :] = jnp.concatenate([values[4:16], zero_four], axis=0).astype(BF16)

    def hidden_body(u, carry):
        summed = cols + rows_scr[pl.ds(u, 1), :]
        value, slope = gelu_and_slope(summed)
        slope_scr[u] = slope
        put_row(hid, u + 1, value)
        return carry

    lax.fori_loop(0, 32, hidden_body, 0)

    out_scale = out_w_ref[...].astype(F32)
    chain_lane = lax.broadcasted_iota(jnp.int32, (CH, CH), 1)

    def conv_pairs(ref, weights, v, count):
        blocks = []
        for c in range(count):
            row = 2 * (v * count + c)
            blocks.append(
                jnp.concatenate(
                    [
                        ref[row + a, 16 * b : 16 * b + 128, :]
                        for a in range(4)
                        for b in range(3)
                    ],
                    axis=1,
                )
            )
        return jnp.dot(jnp.concatenate(blocks, axis=0), weights, preferred_element_type=F32)

    PAIRS = 4

    def forward_body(v, diff):
        conv = conv_pairs(hid, fwd_w[...], v, PAIRS)
        for c in range(PAIRS):
            for e in range(2):
                u = 2 * (v * PAIRS + c) + e
                out = conv[128 * c : 128 * c + 128, CH * e : CH * e + CH]
                value, slope = gelu_and_slope(out)
                summed = (hid[u + 1, 16:144, :].astype(F32) + value) * out_scale
                predicted = jnp.sum(summed, axis=1, keepdims=True)
                wanted = jnp.sum(
                    jnp.where(chain_lane == u, target, 0.0), axis=1, keepdims=True
                )
                direct = ((predicted - wanted) * 0.0625) * out_scale
                direct_scr[u] = direct
                put_row(cgrad, u + 1, direct * slope)
                diff = jnp.where(chain_lane == u, predicted, diff)
        return diff

    predicted = lax.fori_loop(0, 16 // PAIRS, forward_body, jnp.zeros((CH, CH), F32))

    pred_t[...] = jnp.zeros_like(pred_t)
    for q in range(8):
        for s in range(4):
            at = 16 * q + 4 * s
            pred_t[pl.ds(8 * (q + 8 * s) + 4 * half, 4), :] = predicted[at : at + 4]
    home = pred_t[...].T
    for d in range(N_SEQ):
        pred_out_s[d] = home[2 * d : 2 * d + 2]
    send_all(3, lambda peer: pred_out_s.at[peer], pred_in)
    pred_in[pl.ds(me, 1)] = pred_out_s[pl.ds(me, 1)]

    def backward_body(v, colsum):
        conv = conv_pairs(cgrad, bwd_w[...], v, PAIRS)
        for c in range(PAIRS):
            for e in range(2):
                u = 2 * (v * PAIRS + c) + e
                out = conv[128 * c : 128 * c + 128, CH * e : CH * e + CH]
                grad = (direct_scr[u] + out) * slope_scr[u]
                rowsum[pl.ds(u, 1), :] = jnp.sum(grad, axis=0, keepdims=True)
                colsum = colsum + grad
        return colsum

    colsum = lax.fori_loop(0, 16 // PAIRS, backward_body, jnp.zeros((CH, CH), F32))

    for d in range(N_SEQ):
        for e in range(2):
            m = 2 * d + e
            at = 16 * (m % 8) + 4 * (m // 8)
            part_out[d, 4 * e : 4 * e + 4, :] = colsum[at : at + 4]
        part_out[d, 8:10, :] = rowsum[2 * d : 2 * d + 2, :]
        part_out[d, 10:16, :] = jnp.zeros((6, CH), F32)
    send_all(4, lambda peer: part_out.at[peer], part_in)
    part_in[pl.ds(me, 1)] = part_out[pl.ds(me, 1)]

    wait_recv(3, pred_in)
    for r in range(8):
        both = pred_in[2 * r] + pred_in[2 * r + 1]
        pred_ref[r : r + 1, :] = both[0:1]
        pred_ref[r + 8 : r + 9, :] = both[1:2]

    wait_recv(4, part_in)
    col_halves = []
    for h in range(2):
        total = part_in[h, 0:8, :]
        for r in range(1, 8):
            total = total + part_in[2 * r + h, 0:8, :]
        col_halves.append(total)
    col_grad = jnp.concatenate(
        [
            col_halves[0][0:4],
            col_halves[1][0:4],
            col_halves[0][4:8],
            col_halves[1][4:8],
        ],
        axis=0,
    )
    row_pairs = [part_in[2 * r, 8:10, :] + part_in[2 * r + 1, 8:10, :] for r in range(8)]
    row_grad = jnp.concatenate(
        [pair[0:1] for pair in row_pairs] + [pair[1:2] for pair in row_pairs], axis=0
    )
    grads = jnp.concatenate([row_grad, col_grad], axis=1)
    high = grads.astype(BF16)
    rest = grads - high.astype(F32)
    middle = rest.astype(BF16)
    low = (rest - middle.astype(F32)).astype(BF16)
    stacked = jnp.concatenate([high, middle, low], axis=0)
    wide = lax.dot_general(
        stacked,
        jnp.concatenate([row_proj_ref[...], col_proj_ref[...]], axis=1),
        (((1,), (1,)), ((), ())),
        preferred_element_type=F32,
    )
    grad_ref[...] = (wide[32:48] + wide[16:32]) + wide[0:16]

    wait_send(0, tgt_in)
    wait_send(1, stat_in)
    wait_send(2, emb_in)
    wait_send(3, pred_in)
    wait_send(4, part_in)


def per_device(
    bases, stem_weight, conv_weight, row_proj, col_proj, pair_weight, out_weight, targets
):
    vmem = pl.BlockSpec(memory_space=pltpu.VMEM)
    return pl.pallas_call(
        fused,
        out_shape=(
            jax.ShapeDtypeStruct((LOCAL, BINS), F32),
            jax.ShapeDtypeStruct((LOCAL, TRUNK_CH), F32),
        ),
        in_specs=[vmem, vmem, pl.BlockSpec(memory_space=pl.ANY)] + [vmem] * 5,
        out_specs=(vmem, vmem),
        scratch_shapes=[
            pltpu.VMEM((2, 8, POOL), jnp.int32),
            pltpu.VMEM((ROWS + 16, POOL), jnp.int32),
            pltpu.VMEM((264, POOL), jnp.int32),
            pltpu.VMEM((32, STEM_CH), F32),
            pltpu.VMEM((ROWS + 16, STEM_CH), F32),
            pltpu.VMEM((ROWS, 5 * STEM_CH), BF16),
            pltpu.VMEM((TILES, 5 * STEM_CH, 256), BF16),
            pltpu.VMEM((TILES, LOCAL, 256), F32),
            pltpu.VMEM((8, 512), F32),
            pltpu.VMEM((N_SEQ, 8, 512), F32),
            pltpu.VMEM((N_SEQ, 16, CH), F32),
            pltpu.VMEM((N_SEQ, 16, CH), F32),
            pltpu.VMEM((8, 2, BINS), jnp.int32),
            pltpu.VMEM((N_SEQ, 2, BINS), jnp.int32),
            pltpu.VMEM((CH, BINS), F32),
            pltpu.VMEM((BINS, CH), F32),
            pltpu.VMEM((12 * CH, 2 * CH), BF16),
            pltpu.VMEM((12 * CH, 2 * CH), BF16),
            pltpu.VMEM((32, CH), F32),
            pltpu.VMEM((34, 160, CH), BF16),
            pltpu.VMEM((32, CH, CH), F32),
            pltpu.VMEM((32, CH, CH), F32),
            pltpu.VMEM((34, 160, CH), BF16),
            pltpu.VMEM((BINS, CH), F32),
            pltpu.VMEM((N_SEQ, 2, BINS), F32),
            pltpu.VMEM((N_SEQ, 2, BINS), F32),
            pltpu.VMEM((32, CH), F32),
            pltpu.VMEM((N_SEQ, 16, CH), F32),
            pltpu.VMEM((N_SEQ, 16, CH), F32),
            pltpu.SemaphoreType.DMA((TILES,)),
            pltpu.SemaphoreType.DMA((2,)),
            pltpu.SemaphoreType.DMA((2,)),
            pltpu.SemaphoreType.DMA((5,)),
            pltpu.SemaphoreType.DMA((5,)),
        ],
        compiler_params=pltpu.CompilerParams(
            collective_id=0, has_side_effects=True, vmem_limit_bytes=56 << 20
        ),
    )(
        bases.reshape(ROWS, POOL),
        stem_weight,
        conv_weight.reshape(5 * STEM_CH, TRUNK_CH),
        row_proj,
        col_proj,
        pair_weight.reshape(9 * CH, CH),
        out_weight.reshape(1, CH),
        targets,
    )


def solution(mesh):
    in_specs = (P(("dp", "seq")), P(), P(), P(), P(), P(), P(), P(("dp", "seq"), None))
    out_specs = (P(("dp", "seq"), None), P(("dp", "seq"), None))
    return jax.shard_map(
        per_device, mesh=mesh, in_specs=in_specs, out_specs=out_specs, check_vma=False
    )
```

time: 306 us -> 56.4 us (0.18); the launches traced: 302 us -> 56.2 us
  waiting for transfers between devices: 84.7 us -> 0 us
  blocking collectives: 76 us -> 0 us
  matrix products: 72 us -> 0 us
  Pallas kernels: 0 us -> 52.7 us
  starting transfers between devices: 20.6 us -> 0 us
  loops' own time: 15.9 us -> 0 us
  between operations: 14.5 us -> 0.64 us
  other arithmetic: 8.6 us -> 0 us
  local copies, waits for them, and re-layouts: 9.61 us -> 2.86 us
    dot_general x35 -> x0, matrix products: 72 us -> none  [the longest x8 44.9 us: stem_block(): jnp.dot(onehot, stem_weight, preferred_element_type=jnp.float32)]
    reduce_scatter x1 -> x0, waiting for transfers between devices: 65.5 us -> none  [per_device(): lax.psum_scatter(jnp.dot(col_part, col_matrix, precision=lax.Precision.HI...]
    pallas_call x0 -> x1, Pallas kernels: none -> 52.7 us  [per_device(): pl.pallas_call(fused, out_shape=(jax.ShapeDtypeStruct((LOCAL, BINS), F32)...]
    psum x1 -> x0, blocking collectives: 50.9 us -> none  [per_device(): lax.psum((jnp.sum(pooled2, axis=0), jnp.sum(pooled2 * pooled2, axis=0)),...]
    all_gather x1 -> x0, blocking collectives: 25.1 us -> none  [per_device(): lax.all_gather(normed, 'seq', axis=0, tiled=True)]
    ppermute x8 -> x0, starting transfers between devices: 20.6 us -> none  [the longest x4 11.5 us: extended_2(): before = lax.ppermute(last, axis, up)]
    ppermute x8 -> x0, waiting for transfers between devices: 19.2 us -> none  [the longest x4 11.8 us: extended_2(): after = lax.ppermute(leading, axis, down)]
    another operation x1 -> x0, loops' own time: 15.9 us -> none  [per_device(): lax.map(lambda first_row: stem_block(extended_bases, first_row, stem_weig...]
  transfers between devices with their start and end apart: 9 -> 0, of which waited for: 7 -> 0; matrix products, arithmetic and copies ran while one was open for 2% -> 0% of each run, Pallas kernels for 0% -> 0%
where the time goes in v1:
time: 56.4 us; the launch traced here: 56.2 us
  Pallas kernels  52.7 us (93%)
  local copies, waits for them, and re-layouts  2.86 us (5%)
  between operations  0.64 us (1%)
    pallas_call x1, Pallas kernels, per_device(): pl.pallas_call(fused, out_shape=(jax.ShapeDtypeStruct((LOCAL, BINS), F32)...  52.7 us
    unnamed x2, local copies, waits for them, and re-layouts  2.86 us

profile of v1, /device:TPU:1, one launch (start us, length us, event | category | flops | bytes accessed | tf_op | source)
XLA Modules:
  0.0 56.2 jit_solution(16048520363072809684)
XLA Ops:
  0.6 52.7 %shard_map.95 = (f32[16,256]{1,0:T(8,128)}, f32[16,1536]{1,0:T(8,128)}) custom-call(s32[256,128]{1,0:T(8,128)} %bitcast.6, bf16[20,768]{1,0:T(8,128)(2,1)} %stem_ref.1, bf16[3840,1536]{1,0:T(8,128)(2,1)} %bitcast.4, bf16[1536,128]{1,0:T(8,128)(2,1)} %row_proj_ref.1, bf16[1536,128]{1,0:T(8,128)(2,1)} %col_proj_ref.1, bf16[1152,128]{1,0:T(8,128)(2,1)} %bitcast.5, ...), custom_call_target="tpu_custom_call" | custom-call | tf_op jit(solution)/shard_map/pallas_call | solution.py:482
  53.3 1.3 %copy.12 = f32[16,256]{1,0:T(8,128)} copy(f32[16,256]{1,0:T(8,128)} %get-tuple-element.4) | data formatting | bytes 32768
  54.6 1.5 %copy.13 = f32[16,1536]{1,0:T(8,128)} copy(f32[16,1536]{1,0:T(8,128)} %get-tuple-element.5) | data formatting | bytes 196608

commit v2 on v1

--- a/solution.py
+++ b/solution.py
@@ -32,10 +32,10 @@
 
 def gelu_and_slope(x):
     square = x * x
-    t = jnp.tanh(x * (C0 + (C0 * 0.044715) * square))
-    half = 0.5 * x
-    slope = 0.5 + 0.5 * t + half * (1.0 - t * t) * (C0 + (3.0 * C0 * 0.044715) * square)
-    return half + half * t, slope
+    a = 0.5 + 0.5 * jnp.tanh(x * (C0 + (C0 * 0.044715) * square))
+    value = x * a
+    slope = a + value * (1.0 - a) * (2.0 * C0 + (6.0 * C0 * 0.044715) * square)
+    return value, slope
 
 
 def fused(
@@ -44,7 +44,7 @@
     conv_ref,
     row_proj_ref,
     col_proj_ref,
-    pair_ref,
+    pair_hbm,
     out_w_ref,
     targets_ref,
     pred_ref,
@@ -57,12 +57,15 @@
     lhs,
     conv_w,
     pooled2,
+    proj,
+    pair_ref,
+    stat_all,
     stat_out,
     stat_in,
+    late_out,
+    late_in,
     emb_out,
     emb_in,
-    tgt_out,
-    tgt_in,
     tgt_rows,
     tgt_t,
     fwd_w,
@@ -73,12 +76,11 @@
     direct_scr,
     cgrad,
     pred_t,
-    pred_out_s,
-    pred_in,
     rowsum,
     part_out,
     part_in,
     conv_sems,
+    weight_sems,
     halo_send,
     halo_recv,
     send_sems,
@@ -90,10 +92,19 @@
     first = me == 0
     last = me == N_SEQ - 1
 
-    for q in range(TILES):
+    conv_copies = [
         pltpu.make_async_copy(
             conv_ref.at[:, pl.ds(256 * q, 256)], conv_w.at[q], conv_sems.at[q]
-        ).start()
+        )
+        for q in range(TILES)
+    ]
+    weight_copies = [
+        pltpu.make_async_copy(row_proj_ref, proj.at[:, pl.ds(0, CH)], weight_sems.at[0]),
+        pltpu.make_async_copy(col_proj_ref, proj.at[:, pl.ds(CH, CH)], weight_sems.at[1]),
+        pltpu.make_async_copy(pair_hbm, pair_ref, weight_sems.at[2]),
+    ]
+    for copy in conv_copies + weight_copies:
+        copy.start()
 
     barrier = pltpu.get_barrier_semaphore()
 
@@ -106,13 +117,8 @@
 
     ext[...] = jnp.zeros_like(ext)
     ext[8 : 8 + ROWS, :] = bases_ref[...] + 1
-    for r in range(8):
-        tgt_out[r, 0:1, :] = targets_ref[r : r + 1, :]
-        tgt_out[r, 1:2, :] = targets_ref[r + 8 : r + 9, :]
     stem_w[...] = jnp.zeros_like(stem_w)
     stem_w[0:20, :] = stem_ref[...].astype(F32)
-
-    pl.semaphore_wait(barrier, N_SEQ - 1)
 
     def send_all(index, source_of, landing):
         def one(k, carry):
@@ -136,27 +142,6 @@
     def wait_send(index, landing):
         blocks = landing.at[pl.ds(0, N_SEQ - 1)]
         pltpu.make_async_copy(blocks, blocks, send_sems.at[index]).wait()
-
-    up = pltpu.make_async_remote_copy(
-        src_ref=bases_ref.at[pl.ds(ROWS - 8, 8)],
-        dst_ref=halo.at[0],
-        send_sem=halo_send.at[0],
-        recv_sem=halo_recv.at[0],
-        device_id={"seq": lax.rem(me + 1, N_SEQ)},
-        device_id_type=MESH,
-    )
-    down = pltpu.make_async_remote_copy(
-        src_ref=bases_ref.at[pl.ds(0, 8)],
-        dst_ref=halo.at[1],
-        send_sem=halo_send.at[1],
-        recv_sem=halo_recv.at[1],
-        device_id={"seq": lax.rem(me + N_SEQ - 1, N_SEQ)},
-        device_id_type=MESH,
-    )
-    up.start()
-    down.start()
-    send_all(0, lambda peer: tgt_out.at[peer // 2], tgt_in)
-    tgt_in[pl.ds(me, 1)] = tgt_out[pl.ds(rho, 1)]
 
     lane = lax.broadcasted_iota(jnp.int32, (1, POOL), 1)
 
@@ -207,21 +192,46 @@
             )
         return jnp.concatenate(parts, axis=1).astype(BF16).astype(F32)
 
+    up = pltpu.make_async_remote_copy(
+        src_ref=bases_ref.at[pl.ds(ROWS - 8, 8)],
+        dst_ref=halo.at[0],
+        send_sem=halo_send.at[0],
+        recv_sem=halo_recv.at[0],
+        device_id={"seq": lax.rem(me + 1, N_SEQ)},
+        device_id_type=MESH,
+    )
+    down = pltpu.make_async_remote_copy(
+        src_ref=bases_ref.at[pl.ds(0, 8)],
+        dst_ref=halo.at[1],
+        send_sem=halo_send.at[1],
+        recv_sem=halo_recv.at[1],
+        device_id={"seq": lax.rem(me + N_SEQ - 1, N_SEQ)},
+        device_id_type=MESH,
+    )
+
     def stem_body(g, carry):
+        @pl.when(g == 2)
+        def _():
+            pl.semaphore_wait(barrier, N_SEQ - 1)
+            up.start()
+            down.start()
+
+        @pl.when(g == 10)
+        def _():
+            up.wait()
+            down.wait()
+            ext[0:8, :] = jnp.where(first, 0, halo[0] + 1)
+            ext[8 + ROWS : 16 + ROWS, :] = jnp.where(last, 0, halo[1] + 1)
+            codes[240:250, :] = code_rows(6, 10)
+            codes[250:260, :] = code_rows(256, 10)
+            codes[260:264, :] = jnp.zeros((4, POOL), jnp.int32)
+
         start = pl.multiple_of(g * GROUP, 8)
         pooled1[pl.ds(pl.multiple_of(16 + g * GROUP, 8), GROUP), :] = stem_step(start)
         return carry
 
-    lax.fori_loop(0, 10, stem_body, 0)
-
-    up.wait()
-    down.wait()
-    ext[0:8, :] = jnp.where(first, 0, halo[0] + 1)
-    ext[8 + ROWS : 16 + ROWS, :] = jnp.where(last, 0, halo[1] + 1)
-    codes[240:250, :] = code_rows(6, 10)
-    codes[250:260, :] = code_rows(256, 10)
-    codes[260:264, :] = jnp.zeros((4, POOL), jnp.int32)
-    edge = stem_step(240)
+    lax.fori_loop(0, 11, stem_body, 0)
+    edge = pooled1[256:280, :]
     pooled1[6:16, :] = edge[0:10]
     pooled1[256:266, :] = edge[10:20]
     pooled1[6:8, :] = jnp.where(first, 0.0, edge[0:2])
@@ -230,35 +240,44 @@
     for k in range(5):
         lhs[:, STEM_CH * k : STEM_CH * k + STEM_CH] = pooled1[6 + k : 6 + k + ROWS, :].astype(BF16)
 
-    for q in range(TILES):
-        pltpu.make_async_copy(
-            conv_ref.at[:, pl.ds(256 * q, 256)], conv_w.at[q], conv_sems.at[q]
-        ).wait()
-
-    def trunk_body(q, carry):
+    for copy in conv_copies:
+        copy.wait()
+
+    def trunk_tile(q):
         trunk = jnp.dot(lhs[...], conv_w[q], preferred_element_type=F32)
         trunk = trunk.reshape(LOCAL, 16, 256)
-        pooled2[q] = jnp.maximum(
-            gelu(jnp.max(trunk, axis=1)), gelu(jnp.min(trunk, axis=1))
-        )
+        block = jnp.maximum(gelu(jnp.max(trunk, axis=1)), gelu(jnp.min(trunk, axis=1)))
+        pooled2[q] = block
+        total = jnp.sum(block, axis=0, keepdims=True)
+        return total, jnp.sum(block * block, axis=0, keepdims=True)
+
+    def tile(q, carry):
+        total, square = trunk_tile(q)
+        stat_all[pl.ds(q, 1), :] = total
+        stat_all[pl.ds(8 + q, 1), :] = square
+
+        @pl.when(q == 3)
+        def _():
+            stat_out[0:4, :] = stat_all[0:4, :]
+            stat_out[4:8, :] = stat_all[8:12, :]
+            send_all(0, lambda peer: stat_out, stat_in)
+
         return carry
 
-    lax.fori_loop(0, TILES, trunk_body, 0)
-
-    sums = []
-    squares = []
-    for q in range(TILES):
-        block = pooled2[q]
-        sums.append(jnp.sum(block, axis=0, keepdims=True))
-        squares.append(jnp.sum(block * block, axis=0, keepdims=True))
-    for a in range(3):
-        stat_out[a : a + 1, :] = jnp.concatenate(sums[2 * a : 2 * a + 2], axis=1)
-        stat_out[4 + a : 5 + a, :] = jnp.concatenate(squares[2 * a : 2 * a + 2], axis=1)
-    stat_out[3:4, :] = jnp.zeros((1, 512), F32)
-    stat_out[7:8, :] = jnp.zeros((1, 512), F32)
-    send_all(1, lambda peer: stat_out, stat_in)
+    lax.fori_loop(0, TILES, tile, 0)
     stat_in[pl.ds(me, 1)] = stat_out[...][None]
-
+    for r in range(8):
+        late_out[r, 0:2, :] = stat_all[4:6, :]
+        late_out[r, 2:4, :] = stat_all[12:14, :]
+    for r in range(8):
+        for e in range(2):
+            late_out[r, 4 + e : 5 + e, :] = targets_ref[r + 8 * e : r + 8 * e + 1, :].astype(F32)
+        late_out[r, 6:8, :] = jnp.zeros((2, 256), F32)
+    send_all(1, lambda peer: late_out.at[peer // 2], late_in)
+    late_in[pl.ds(me, 1)] = late_out[pl.ds(rho, 1)]
+
+    for copy in weight_copies:
+        copy.wait()
     zero_block = jnp.zeros((CH, CH), BF16)
     for a in range(4):
         for b in range(3):
@@ -282,45 +301,27 @@
             )
             bwd_w[at : at + CH, :] = jnp.concatenate([near, far], axis=1)
 
-    wait_recv(0, tgt_in)
-    tgt_rows[...] = jnp.zeros_like(tgt_rows)
-    for d in range(N_SEQ):
-        tgt_rows[2 * d : 2 * d + 2, :] = tgt_in[d].astype(F32)
-    tgt_t[...] = tgt_rows[...].T
-
-    def chain_order(load):
-        pieces = []
-        for q in range(8):
-            for s in range(4):
-                pieces.append(load(q + 8 * s))
-        return jnp.concatenate(pieces, axis=0)
-
-    target = chain_order(lambda m: tgt_t[pl.ds(8 * m + 4 * half, 4), :])
-    target = (target - 7.5) * 0.25
-
-    zero_tile = jnp.zeros((16, CH), BF16)
     zero_row = jnp.zeros((160, CH), BF16)
     hid[0] = zero_row
     hid[33] = zero_row
     cgrad[0] = zero_row
     cgrad[33] = zero_row
 
-    wait_recv(1, stat_in)
-    total = jnp.sum(stat_in[...], axis=0)
-    mean = total[0:4] / BINS
-    var = total[4:8] / BINS - mean * mean
+    wait_recv(0, stat_in)
+    early = jnp.sum(stat_in[...], axis=0)
+    wait_recv(1, late_in)
+    late = jnp.sum(late_in[...], axis=0)
+    mean = jnp.concatenate([early[0:4], late[0:2]], axis=0) / BINS
+    var = jnp.concatenate([early[4:8], late[2:4]], axis=0) / BINS - mean * mean
     scale = lax.rsqrt(var + 1e-05)
-    normed = []
-    for q in range(TILES):
-        a, c = q // 2, 256 * (q % 2)
-        normed.append(
-            ((pooled2[q] - mean[a : a + 1, c : c + 256]) * scale[a : a + 1, c : c + 256]).astype(
-                BF16
-            )
-        )
-    normed = jnp.concatenate(normed, axis=1)
-    proj = jnp.concatenate([row_proj_ref[...], col_proj_ref[...]], axis=1)
-    emb = jnp.dot(normed, proj, preferred_element_type=F32).astype(BF16).astype(F32)
+    normed = jnp.concatenate(
+        [
+            ((pooled2[q] - mean[q : q + 1]) * scale[q : q + 1]).astype(BF16)
+            for q in range(TILES)
+        ],
+        axis=1,
+    )
+    emb = jnp.dot(normed, proj[...], preferred_element_type=F32).astype(BF16).astype(F32)
     rows_emb = emb[:, 0:CH]
     cols_emb = emb[:, CH : 2 * CH]
     for h in range(2):
@@ -332,6 +333,22 @@
             emb_out[2 * r + h, 10:16, :] = jnp.zeros((6, CH), F32)
     send_all(2, lambda peer: emb_out.at[peer], emb_in)
     emb_in[pl.ds(me, 1)] = emb_out[pl.ds(me, 1)]
+
+    tgt_rows[...] = jnp.zeros_like(tgt_rows)
+    for d in range(N_SEQ):
+        tgt_rows[2 * d : 2 * d + 2, :] = late_in[d, 4:6, :]
+    tgt_t[...] = tgt_rows[...].T
+
+    def chain_order(load):
+        pieces = []
+        for q in range(8):
+            for s in range(4):
+                pieces.append(load(q + 8 * s))
+        return jnp.concatenate(pieces, axis=0)
+
+    target = chain_order(lambda m: tgt_t[pl.ds(8 * m + 4 * half, 4), :])
+    target = (target - 7.5) * 0.25
+
     wait_recv(2, emb_in)
 
     for d in range(N_SEQ):
@@ -351,9 +368,10 @@
         put_row(hid, u + 1, value)
         return carry
 
-    lax.fori_loop(0, 32, hidden_body, 0)
+    lax.fori_loop(0, 32, hidden_body, 0, unroll=4)
 
     out_scale = out_w_ref[...].astype(F32)
+    small_scale = out_scale * (1.0 / math.sqrt(BINS))
     chain_lane = lax.broadcasted_iota(jnp.int32, (CH, CH), 1)
 
     def conv_pairs(ref, weights, v, count):
@@ -372,7 +390,7 @@
             )
         return jnp.dot(jnp.concatenate(blocks, axis=0), weights, preferred_element_type=F32)
 
-    PAIRS = 4
+    PAIRS = 8
 
     def forward_body(v, diff):
         conv = conv_pairs(hid, fwd_w[...], v, PAIRS)
@@ -382,28 +400,16 @@
                 out = conv[128 * c : 128 * c + 128, CH * e : CH * e + CH]
                 value, slope = gelu_and_slope(out)
                 summed = (hid[u + 1, 16:144, :].astype(F32) + value) * out_scale
-                predicted = jnp.sum(summed, axis=1, keepdims=True)
-                wanted = jnp.sum(
-                    jnp.where(chain_lane == u, target, 0.0), axis=1, keepdims=True
-                )
-                direct = ((predicted - wanted) * 0.0625) * out_scale
+                summed = summed - jnp.where(chain_lane == u, target, 0.0)
+                error = jnp.sum(summed, axis=1, keepdims=True)
+                direct = error * small_scale
                 direct_scr[u] = direct
                 put_row(cgrad, u + 1, direct * slope)
-                diff = jnp.where(chain_lane == u, predicted, diff)
+                diff = jnp.where(chain_lane == u, error, diff)
         return diff
 
-    predicted = lax.fori_loop(0, 16 // PAIRS, forward_body, jnp.zeros((CH, CH), F32))
-
-    pred_t[...] = jnp.zeros_like(pred_t)
-    for q in range(8):
-        for s in range(4):
-            at = 16 * q + 4 * s
-            pred_t[pl.ds(8 * (q + 8 * s) + 4 * half, 4), :] = predicted[at : at + 4]
-    home = pred_t[...].T
-    for d in range(N_SEQ):
-        pred_out_s[d] = home[2 * d : 2 * d + 2]
-    send_all(3, lambda peer: pred_out_s.at[peer], pred_in)
-    pred_in[pl.ds(me, 1)] = pred_out_s[pl.ds(me, 1)]
+    errors = lax.fori_loop(0, 16 // PAIRS, forward_body, jnp.zeros((CH, CH), F32))
+    predicted = errors + target
 
     def backward_body(v, colsum):
         conv = conv_pairs(cgrad, bwd_w[...], v, PAIRS)
@@ -418,23 +424,30 @@
 
     colsum = lax.fori_loop(0, 16 // PAIRS, backward_body, jnp.zeros((CH, CH), F32))
 
+    pred_t[...] = jnp.zeros_like(pred_t)
+    for q in range(8):
+        for s in range(4):
+            at = 16 * q + 4 * s
+            pred_t[pl.ds(8 * (q + 8 * s) + 4 * half, 4), :] = predicted[at : at + 4]
+    home = pred_t[...].T
     for d in range(N_SEQ):
         for e in range(2):
             m = 2 * d + e
             at = 16 * (m % 8) + 4 * (m // 8)
             part_out[d, 4 * e : 4 * e + 4, :] = colsum[at : at + 4]
+            part_out[d, 10 + e : 11 + e, :] = home[m : m + 1, 0:CH]
+            part_out[d, 12 + e : 13 + e, :] = home[m : m + 1, CH : 2 * CH]
         part_out[d, 8:10, :] = rowsum[2 * d : 2 * d + 2, :]
-        part_out[d, 10:16, :] = jnp.zeros((6, CH), F32)
-    send_all(4, lambda peer: part_out.at[peer], part_in)
+        part_out[d, 14:16, :] = jnp.zeros((2, CH), F32)
+    send_all(3, lambda peer: part_out.at[peer], part_in)
     part_in[pl.ds(me, 1)] = part_out[pl.ds(me, 1)]
 
-    wait_recv(3, pred_in)
+    wait_recv(3, part_in)
     for r in range(8):
-        both = pred_in[2 * r] + pred_in[2 * r + 1]
-        pred_ref[r : r + 1, :] = both[0:1]
-        pred_ref[r + 8 : r + 9, :] = both[1:2]
-
-    wait_recv(4, part_in)
+        both = part_in[2 * r, 10:14, :] + part_in[2 * r + 1, 10:14, :]
+        for e in range(2):
+            pred_ref[r + 8 * e : r + 8 * e + 1, 0:CH] = both[e : e + 1]
+            pred_ref[r + 8 * e : r + 8 * e + 1, CH : 2 * CH] = both[2 + e : 3 + e]
     col_halves = []
     for h in range(2):
         total = part_in[h, 0:8, :]
@@ -462,46 +475,49 @@
     stacked = jnp.concatenate([high, middle, low], axis=0)
     wide = lax.dot_general(
         stacked,
-        jnp.concatenate([row_proj_ref[...], col_proj_ref[...]], axis=1),
+        proj[...],
         (((1,), (1,)), ((), ())),
         preferred_element_type=F32,
     )
     grad_ref[...] = (wide[32:48] + wide[16:32]) + wide[0:16]
 
-    wait_send(0, tgt_in)
-    wait_send(1, stat_in)
+    wait_send(0, stat_in)
+    wait_send(1, late_in)
     wait_send(2, emb_in)
-    wait_send(3, pred_in)
-    wait_send(4, part_in)
+    wait_send(3, part_in)
 
 
 def per_device(
     bases, stem_weight, conv_weight, row_proj, col_proj, pair_weight, out_weight, targets
 ):
     vmem = pl.BlockSpec(memory_space=pltpu.VMEM)
+    hbm = pl.BlockSpec(memory_space=pl.ANY)
     return pl.pallas_call(
         fused,
         out_shape=(
             jax.ShapeDtypeStruct((LOCAL, BINS), F32),
             jax.ShapeDtypeStruct((LOCAL, TRUNK_CH), F32),
         ),
-        in_specs=[vmem, vmem, pl.BlockSpec(memory_space=pl.ANY)] + [vmem] * 5,
+        in_specs=[vmem, vmem, hbm, hbm, hbm, hbm, vmem, vmem],
         out_specs=(vmem, vmem),
         scratch_shapes=[
             pltpu.VMEM((2, 8, POOL), jnp.int32),
             pltpu.VMEM((ROWS + 16, POOL), jnp.int32),
             pltpu.VMEM((264, POOL), jnp.int32),
             pltpu.VMEM((32, STEM_CH), F32),
-            pltpu.VMEM((ROWS + 16, STEM_CH), F32),
+            pltpu.VMEM((ROWS + 24, STEM_CH), F32),
             pltpu.VMEM((ROWS, 5 * STEM_CH), BF16),
             pltpu.VMEM((TILES, 5 * STEM_CH, 256), BF16),
             pltpu.VMEM((TILES, LOCAL, 256), F32),
-            pltpu.VMEM((8, 512), F32),
-            pltpu.VMEM((N_SEQ, 8, 512), F32),
+            pltpu.VMEM((TRUNK_CH, 2 * CH), BF16),
+            pltpu.VMEM((9 * CH, CH), BF16),
+            pltpu.VMEM((16, 256), F32),
+            pltpu.VMEM((8, 256), F32),
+            pltpu.VMEM((N_SEQ, 8, 256), F32),
+            pltpu.VMEM((8, 8, 256), F32),
+            pltpu.VMEM((N_SEQ, 8, 256), F32),
             pltpu.VMEM((N_SEQ, 16, CH), F32),
             pltpu.VMEM((N_SEQ, 16, CH), F32),
-            pltpu.VMEM((8, 2, BINS), jnp.int32),
-            pltpu.VMEM((N_SEQ, 2, BINS), jnp.int32),
             pltpu.VMEM((CH, BINS), F32),
             pltpu.VMEM((BINS, CH), F32),
             pltpu.VMEM((12 * CH, 2 * CH), BF16),
@@ -512,16 +528,15 @@
             pltpu.VMEM((32, CH, CH), F32),
             pltpu.VMEM((34, 160, CH), BF16),
             pltpu.VMEM((BINS, CH), F32),
-            pltpu.VMEM((N_SEQ, 2, BINS), F32),
-            pltpu.VMEM((N_SEQ, 2, BINS), F32),
             pltpu.VMEM((32, CH), F32),
             pltpu.VMEM((N_SEQ, 16, CH), F32),
             pltpu.VMEM((N_SEQ, 16, CH), F32),
             pltpu.SemaphoreType.DMA((TILES,)),
+            pltpu.SemaphoreType.DMA((3,)),
             pltpu.SemaphoreType.DMA((2,)),
             pltpu.SemaphoreType.DMA((2,)),
-            pltpu.SemaphoreType.DMA((5,)),
-            pltpu.SemaphoreType.DMA((5,)),
+            pltpu.SemaphoreType.DMA((4,)),
+            pltpu.SemaphoreType.DMA((4,)),
         ],
         compiler_params=pltpu.CompilerParams(
             collective_id=0, has_side_effects=True, vmem_limit_bytes=56 << 20

time: 56.4 us -> 52 us (0.922)
  Pallas kernels: 52.7 us -> 48.3 us
    pallas_call x1, Pallas kernels: 52.7 us -> 48.3 us  [per_device(): pl.pallas_call(fused, out_shape=(jax.ShapeDtypeStruct((LOCAL, BINS), F32)...]
where the time goes in v2:
time: 52 us; the launch traced here: 51.8 us
  Pallas kernels  48.3 us (93%)
  local copies, waits for them, and re-layouts  2.86 us (6%)
  between operations  0.64 us (1%)
    pallas_call x1, Pallas kernels, per_device(): pl.pallas_call(fused, out_shape=(jax.ShapeDtypeStruct((LOCAL, BINS), F32)...  48.3 us
    unnamed x2, local copies, waits for them, and re-layouts  2.86 us

profile of v2, /device:TPU:1, one launch (start us, length us, event | category | flops | bytes accessed | tf_op | source)
XLA Modules:
  0.0 51.8 jit_solution(13760241213822284142)
XLA Ops:
  0.6 48.3 %shard_map.95 = (f32[16,256]{1,0:T(8,128)}, f32[16,1536]{1,0:T(8,128)}) custom-call(s32[256,128]{1,0:T(8,128)} %bitcast.6, bf16[20,768]{1,0:T(8,128)(2,1)} %stem_ref.1, bf16[3840,1536]{1,0:T(8,128)(2,1)} %bitcast.4, bf16[1536,128]{1,0:T(8,128)(2,1)} %row_proj_ref.1, bf16[1536,128]{1,0:T(8,128)(2,1)} %col_proj_ref.1, bf16[1152,128]{1,0:T(8,128)(2,1)} %bitcast.5, ...), custom_call_target="tpu_custom_call" | custom-call | tf_op jit(solution)/shard_map/pallas_call | solution.py:495
  48.9 1.3 %copy.12 = f32[16,256]{1,0:T(8,128)} copy(f32[16,256]{1,0:T(8,128)} %get-tuple-element.4) | data formatting | bytes 32768
  50.3 1.5 %copy.13 = f32[16,1536]{1,0:T(8,128)} copy(f32[16,1536]{1,0:T(8,128)} %get-tuple-element.5) | data formatting | bytes 196608

commit v3 on v2

--- a/solution.py
+++ b/solution.py
@@ -9,6 +9,10 @@
 from jax.sharding import PartitionSpec as P
 
 MESH = pl.DeviceIdType.MESH
+FAR_FIRST = sorted(
+    [(z, x, c) for z in range(2) for x in range(4) for c in range(2) if (z, x, c) != (0, 0, 0)],
+    key=lambda d: -(d[0] + min(d[1], 4 - d[1]) + 0.1 * d[2]),
+)
 F32 = jnp.float32
 BF16 = jnp.bfloat16
 
@@ -20,6 +24,7 @@
 ROWS = 256
 BINS = 256
 LOCAL = 16
+OFF = 32
 GROUP = 24
 TILES = TRUNK_CH // 256
 C0 = math.sqrt(2.0 / math.pi)
@@ -39,20 +44,26 @@
 
 
 def fused(
-    bases_ref,
-    stem_ref,
+    bases_hbm,
+    stem_hbm,
     conv_ref,
     row_proj_ref,
     col_proj_ref,
     pair_hbm,
+    out_w_hbm,
+    targets_hbm,
+    pred_ref,
+    grad_ref,
+    bases_ref,
+    stem_ref,
     out_w_ref,
     targets_ref,
-    pred_ref,
-    grad_ref,
     halo,
     ext,
     codes,
     stem_w,
+    onehot,
+    extremes,
     pooled1,
     lhs,
     conv_w,
@@ -79,6 +90,7 @@
     rowsum,
     part_out,
     part_in,
+    input_sems,
     conv_sems,
     weight_sems,
     halo_send,
@@ -89,9 +101,18 @@
     me = lax.axis_index("seq")
     rho = me // 2
     half = me % 2
+    z, x, core = me // 8, lax.rem(me // 2, 4), half
     first = me == 0
     last = me == N_SEQ - 1
 
+    input_copies = [
+        pltpu.make_async_copy(bases_hbm, bases_ref, input_sems.at[0]),
+        pltpu.make_async_copy(stem_hbm, stem_ref, input_sems.at[1]),
+        pltpu.make_async_copy(out_w_hbm, out_w_ref, input_sems.at[2]),
+        pltpu.make_async_copy(targets_hbm, targets_ref, input_sems.at[3]),
+    ]
+    for copy in input_copies:
+        copy.start()
     conv_copies = [
         pltpu.make_async_copy(
             conv_ref.at[:, pl.ds(256 * q, 256)], conv_w.at[q], conv_sems.at[q]
@@ -103,8 +124,6 @@
         pltpu.make_async_copy(col_proj_ref, proj.at[:, pl.ds(CH, CH)], weight_sems.at[1]),
         pltpu.make_async_copy(pair_hbm, pair_ref, weight_sems.at[2]),
     ]
-    for copy in conv_copies + weight_copies:
-        copy.start()
 
     barrier = pltpu.get_barrier_semaphore()
 
@@ -116,13 +135,15 @@
     lax.fori_loop(1, N_SEQ, greet, 0)
 
     ext[...] = jnp.zeros_like(ext)
+    for copy in input_copies:
+        copy.wait()
     ext[8 : 8 + ROWS, :] = bases_ref[...] + 1
     stem_w[...] = jnp.zeros_like(stem_w)
     stem_w[0:20, :] = stem_ref[...].astype(F32)
 
     def send_all(index, source_of, landing):
-        def one(k, carry):
-            peer = lax.rem(me + k, N_SEQ)
+        for dz, dx, dc in FAR_FIRST:
+            peer = 8 * lax.rem(z + dz, 2) + 2 * lax.rem(x + dx, 4) + lax.rem(core + dc, 2)
             pltpu.make_async_remote_copy(
                 src_ref=source_of(peer),
                 dst_ref=landing.at[me],
@@ -131,9 +152,6 @@
                 device_id={"seq": peer},
                 device_id_type=MESH,
             ).start()
-            return carry
-
-        lax.fori_loop(1, N_SEQ, one, 0)
 
     def wait_recv(index, landing):
         blocks = landing.at[pl.ds(0, N_SEQ - 1)]
@@ -169,28 +187,17 @@
     tap_shift = (sub >> 2) * 3
     zero_rows = jnp.zeros((8, POOL), F32)
 
-    def stem_step(start):
-        pieces = []
-        for r in range(GROUP):
-            code = jnp.broadcast_to(codes[pl.ds(start + r, 1), :], (8, POOL))
-            taps = [
-                jnp.where(((code >> (tap_shift + 6 * k)) & 7) == base_code, 1.0, 0.0).astype(F32)
-                for k in range(3)
-            ]
-            pieces.append(jnp.concatenate(taps + [zero_rows], axis=0).astype(BF16))
-        onehot = jnp.concatenate(pieces, axis=1)
-        parts = []
-        for n in range(STEM_CH // 256):
-            stem = lax.dot_general(
-                onehot,
-                stem_w[:, 256 * n : 256 * n + 256].astype(BF16),
-                (((0,), (0,)), ((), ())),
-                preferred_element_type=F32,
-            ).reshape(GROUP, POOL, 256)
-            parts.append(
-                jnp.maximum(gelu(jnp.max(stem, axis=1)), gelu(jnp.min(stem, axis=1)))
-            )
-        return jnp.concatenate(parts, axis=1).astype(BF16).astype(F32)
+    def onehot_rows(start, r):
+        code = jnp.broadcast_to(codes[pl.ds(start + r, 1), :], (8, POOL))
+        taps = [
+            jnp.where(((code >> (tap_shift + 6 * k)) & 7) == base_code, 1.0, 0.0).astype(F32)
+            for k in range(3)
+        ]
+        return jnp.concatenate(taps + [zero_rows], axis=0).astype(BF16).T
+
+    def pooled_rows():
+        values = jnp.maximum(gelu(extremes[0]), gelu(extremes[1]))
+        return values.astype(BF16).astype(F32)
 
     up = pltpu.make_async_remote_copy(
         src_ref=bases_ref.at[pl.ds(ROWS - 8, 8)],
@@ -209,14 +216,23 @@
         device_id_type=MESH,
     )
 
+    def first_onehot(r, carry):
+        onehot[0, pl.ds(pl.multiple_of(POOL * r, POOL), POOL), :] = onehot_rows(0, r)
+        return carry
+
+    lax.fori_loop(0, GROUP, first_onehot, 0, unroll=12)
+    extremes[...] = jnp.zeros_like(extremes)
+
     def stem_body(g, carry):
         @pl.when(g == 2)
         def _():
             pl.semaphore_wait(barrier, N_SEQ - 1)
             up.start()
             down.start()
-
-        @pl.when(g == 10)
+            for copy in conv_copies + weight_copies:
+                copy.start()
+
+        @pl.when(g == 9)
         def _():
             up.wait()
             down.wait()
@@ -226,19 +242,30 @@
             codes[250:260, :] = code_rows(256, 10)
             codes[260:264, :] = jnp.zeros((4, POOL), jnp.int32)
 
-        start = pl.multiple_of(g * GROUP, 8)
-        pooled1[pl.ds(pl.multiple_of(16 + g * GROUP, 8), GROUP), :] = stem_step(start)
+        slot = lax.rem(g, 2)
+        pooled1[pl.ds(pl.multiple_of(OFF - 16 + g * GROUP, 8), GROUP), :] = pooled_rows()
+        for n in range(STEM_CH // 256):
+            stem = jnp.dot(
+                onehot[slot],
+                stem_w[:, 256 * n : 256 * n + 256].astype(BF16),
+                preferred_element_type=F32,
+            ).reshape(GROUP, POOL, 256)
+            extremes[0, :, 256 * n : 256 * n + 256] = jnp.max(stem, axis=1)
+            extremes[1, :, 256 * n : 256 * n + 256] = jnp.min(stem, axis=1)
+        start = pl.multiple_of(jnp.minimum(g + 1, 10) * GROUP, 8)
+        for r in range(GROUP):
+            onehot[1 - slot, POOL * r : POOL * r + POOL, :] = onehot_rows(start, r)
         return carry
 
     lax.fori_loop(0, 11, stem_body, 0)
-    edge = pooled1[256:280, :]
-    pooled1[6:16, :] = edge[0:10]
-    pooled1[256:266, :] = edge[10:20]
-    pooled1[6:8, :] = jnp.where(first, 0.0, edge[0:2])
-    pooled1[264:266, :] = jnp.where(last, 0.0, edge[18:20])
+    edge = pooled_rows()
+    pooled1[OFF - 2 : OFF + 8, :] = edge[0:10]
+    pooled1[OFF + 248 : OFF + 258, :] = edge[10:20]
+    pooled1[OFF - 2 : OFF, :] = jnp.where(first, 0.0, edge[0:2])
+    pooled1[OFF + 256 : OFF + 258, :] = jnp.where(last, 0.0, edge[18:20])
 
     for k in range(5):
-        lhs[:, STEM_CH * k : STEM_CH * k + STEM_CH] = pooled1[6 + k : 6 + k + ROWS, :].astype(BF16)
+        lhs[:, STEM_CH * k : STEM_CH * k + STEM_CH] = pooled1[OFF - 2 + k : OFF - 2 + k + ROWS, :].astype(BF16)
 
     for copy in conv_copies:
         copy.wait()
@@ -251,20 +278,14 @@
         total = jnp.sum(block, axis=0, keepdims=True)
         return total, jnp.sum(block * block, axis=0, keepdims=True)
 
-    def tile(q, carry):
+    for q in range(TILES):
         total, square = trunk_tile(q)
-        stat_all[pl.ds(q, 1), :] = total
-        stat_all[pl.ds(8 + q, 1), :] = square
-
-        @pl.when(q == 3)
-        def _():
+        stat_all[q : q + 1, :] = total
+        stat_all[8 + q : 9 + q, :] = square
+        if q == 3:
             stat_out[0:4, :] = stat_all[0:4, :]
             stat_out[4:8, :] = stat_all[8:12, :]
             send_all(0, lambda peer: stat_out, stat_in)
-
-        return carry
-
-    lax.fori_loop(0, TILES, tile, 0)
     stat_in[pl.ds(me, 1)] = stat_out[...][None]
     for r in range(8):
         late_out[r, 0:2, :] = stat_all[4:6, :]
@@ -487,25 +508,37 @@
     wait_send(3, part_in)
 
 
+def deliver(pred_in, grad_in, pred_out, grad_out):
+    pred_out[...] = pred_in[...]
+    grad_out[...] = grad_in[...]
+
+
 def per_device(
     bases, stem_weight, conv_weight, row_proj, col_proj, pair_weight, out_weight, targets
 ):
     vmem = pl.BlockSpec(memory_space=pltpu.VMEM)
     hbm = pl.BlockSpec(memory_space=pl.ANY)
-    return pl.pallas_call(
+    shapes = (
+        jax.ShapeDtypeStruct((LOCAL, BINS), F32),
+        jax.ShapeDtypeStruct((LOCAL, TRUNK_CH), F32),
+    )
+    results = pl.pallas_call(
         fused,
-        out_shape=(
-            jax.ShapeDtypeStruct((LOCAL, BINS), F32),
-            jax.ShapeDtypeStruct((LOCAL, TRUNK_CH), F32),
-        ),
-        in_specs=[vmem, vmem, hbm, hbm, hbm, hbm, vmem, vmem],
+        out_shape=shapes,
+        in_specs=[hbm] * 8,
         out_specs=(vmem, vmem),
         scratch_shapes=[
+            pltpu.VMEM((ROWS, POOL), jnp.int32),
+            pltpu.VMEM((20, STEM_CH), BF16),
+            pltpu.VMEM((1, CH), BF16),
+            pltpu.VMEM((LOCAL, BINS), jnp.int32),
             pltpu.VMEM((2, 8, POOL), jnp.int32),
             pltpu.VMEM((ROWS + 16, POOL), jnp.int32),
             pltpu.VMEM((264, POOL), jnp.int32),
             pltpu.VMEM((32, STEM_CH), F32),
-            pltpu.VMEM((ROWS + 24, STEM_CH), F32),
+            pltpu.VMEM((2, GROUP * POOL, 32), BF16),
+            pltpu.VMEM((2, GROUP, STEM_CH), F32),
+            pltpu.VMEM((OFF + ROWS + 16, STEM_CH), F32),
             pltpu.VMEM((ROWS, 5 * STEM_CH), BF16),
             pltpu.VMEM((TILES, 5 * STEM_CH, 256), BF16),
             pltpu.VMEM((TILES, LOCAL, 256), F32),
@@ -531,6 +564,7 @@
             pltpu.VMEM((32, CH), F32),
             pltpu.VMEM((N_SEQ, 16, CH), F32),
             pltpu.VMEM((N_SEQ, 16, CH), F32),
+            pltpu.SemaphoreType.DMA((4,)),
             pltpu.SemaphoreType.DMA((TILES,)),
             pltpu.SemaphoreType.DMA((3,)),
             pltpu.SemaphoreType.DMA((2,)),
@@ -551,6 +585,9 @@
         out_weight.reshape(1, CH),
         targets,
     )
+    return pl.pallas_call(
+        deliver, out_shape=shapes, in_specs=[vmem, vmem], out_specs=(vmem, vmem)
+    )(*results)
 
 
 def solution(mesh):

time: 52 us -> 47.8 us (0.919)
  local copies, waits for them, and re-layouts: 2.86 us -> 0 us
  Pallas kernels: 48.3 us -> 46.9 us
    unnamed x2 -> x0, local copies, waits for them, and re-layouts: 2.86 us -> none
    pallas_call x1 -> x2, Pallas kernels: 48.3 us -> 46.9 us  [the longest x1 45.4 us: per_device(): pl.pallas_call(fused, out_shape=shapes, in_specs=[hbm] * 8, out_specs=(vm...]
where the time goes in v3:
time: 47.8 us; the launch traced here: 47.6 us
  Pallas kernels  46.9 us (98%)
  between operations  0.64 us (1%)
    pallas_call x1, Pallas kernels, per_device(): pl.pallas_call(fused, out_shape=shapes, in_specs=[hbm] * 8, out_specs=(vm...  45.4 us
    pallas_call x1, Pallas kernels, per_device(): pl.pallas_call(deliver, out_shape=shapes, in_specs=[vmem, vmem], out_spec...  1.56 us

profile of v3, /device:TPU:1, one launch (start us, length us, event | category | flops | bytes accessed | tf_op | source)
XLA Modules:
  0.0 47.6 jit_solution(4061047415401990194)
XLA Ops:
  0.6 45.4 %shard_map.95 = (f32[16,256]{1,0:T(8,128)}, f32[16,1536]{1,0:T(8,128)}) custom-call(s32[256,128]{1,0:T(8,128)} %bitcast.6, bf16[20,768]{1,0:T(8,128)(2,1)} %stem_hbm.1, bf16[3840,1536]{1,0:T(8,128)(2,1)} %bitcast.4, bf16[1536,128]{1,0:T(8,128)(2,1)} %row_proj_ref.1, bf16[1536,128]{1,0:T(8,128)(2,1)} %col_proj_ref.1, bf16[1152,128]{1,0:T(8,128)(2,1)} %bitcast.5, ...), custom_call_target="tpu_custom_call" | custom-call | tf_op jit(solution)/shard_map/pallas_call | solution.py:525
  46.0 1.6 %shard_map.96 = (f32[16,256]{1,0:T(8,128)}, f32[16,1536]{1,0:T(8,128)}) custom-call(f32[16,256]{1,0:T(8,128)} %get-tuple-element.4.pred_in, f32[16,1536]{1,0:T(8,128)} %get-tuple-element.5.grad_in), custom_call_target="tpu_custom_call" | custom-call | tf_op jit(solution)/shard_map/pallas_call | solution.py:588

commit v4 on v3

--- a/solution.py
+++ b/solution.py
@@ -24,7 +24,6 @@
 ROWS = 256
 BINS = 256
 LOCAL = 16
-OFF = 32
 GROUP = 24
 TILES = TRUNK_CH // 256
 C0 = math.sqrt(2.0 / math.pi)
@@ -60,12 +59,13 @@
     targets_ref,
     halo,
     ext,
+    codes_in_order,
     codes,
     stem_w,
     onehot,
     extremes,
     pooled1,
-    lhs,
+    taps,
     conv_w,
     pooled2,
     proj,
@@ -180,7 +180,9 @@
             total = total + (before << (3 * (2 - shift))) + (after << (3 * (2 + shift)))
         return total
 
-    codes[0:240, :] = code_rows(16, 240)
+    codes_in_order[...] = code_rows(8, ROWS)
+    for q in range(1, 15):
+        codes[16 * (q - 1) : 16 * q, :] = codes_in_order[pl.ds(q, 16, stride=16), :]
 
     sub = lax.broadcasted_iota(jnp.int32, (8, POOL), 0)
     base_code = (sub & 3) + 1
@@ -189,11 +191,11 @@
 
     def onehot_rows(start, r):
         code = jnp.broadcast_to(codes[pl.ds(start + r, 1), :], (8, POOL))
-        taps = [
+        pairs = [
             jnp.where(((code >> (tap_shift + 6 * k)) & 7) == base_code, 1.0, 0.0).astype(F32)
             for k in range(3)
         ]
-        return jnp.concatenate(taps + [zero_rows], axis=0).astype(BF16).T
+        return jnp.concatenate(pairs + [zero_rows], axis=0).astype(BF16).T
 
     def pooled_rows():
         values = jnp.maximum(gelu(extremes[0]), gelu(extremes[1]))
@@ -232,18 +234,29 @@
             for copy in conv_copies + weight_copies:
                 copy.start()
 
-        @pl.when(g == 9)
+        @pl.when(g == 8)
         def _():
             up.wait()
             down.wait()
             ext[0:8, :] = jnp.where(first, 0, halo[0] + 1)
             ext[8 + ROWS : 16 + ROWS, :] = jnp.where(last, 0, halo[1] + 1)
-            codes[240:250, :] = code_rows(6, 10)
-            codes[250:260, :] = code_rows(256, 10)
+            begin = code_rows(6, 3)
+            end = code_rows(7 + ROWS, 3)
+            codes_in_order[0:1, :] = begin[2:3]
+            codes_in_order[ROWS - 1 : ROWS, :] = end[0:1]
+            codes[224:240, :] = codes_in_order[pl.ds(0, 16, stride=16), :]
+            codes[240:256, :] = codes_in_order[pl.ds(15, 16, stride=16), :]
+            codes[256:258, :] = begin[0:2]
+            codes[258:260, :] = end[1:3]
             codes[260:264, :] = jnp.zeros((4, POOL), jnp.int32)
 
+        @pl.when(g == 10)
+        def _():
+            for copy in conv_copies:
+                copy.wait()
+
         slot = lax.rem(g, 2)
-        pooled1[pl.ds(pl.multiple_of(OFF - 16 + g * GROUP, 8), GROUP), :] = pooled_rows()
+        pooled1[pl.ds(pl.multiple_of(g * GROUP, 8), GROUP), :] = pooled_rows()
         for n in range(STEM_CH // 256):
             stem = jnp.dot(
                 onehot[slot],
@@ -258,22 +271,36 @@
         return carry
 
     lax.fori_loop(0, 11, stem_body, 0)
-    edge = pooled_rows()
-    pooled1[OFF - 2 : OFF + 8, :] = edge[0:10]
-    pooled1[OFF + 248 : OFF + 258, :] = edge[10:20]
-    pooled1[OFF - 2 : OFF, :] = jnp.where(first, 0.0, edge[0:2])
-    pooled1[OFF + 256 : OFF + 258, :] = jnp.where(last, 0.0, edge[18:20])
-
-    for k in range(5):
-        lhs[:, STEM_CH * k : STEM_CH * k + STEM_CH] = pooled1[OFF - 2 + k : OFF - 2 + k + ROWS, :].astype(BF16)
-
-    for copy in conv_copies:
-        copy.wait()
+    pooled1[11 * GROUP : 12 * GROUP, :] = pooled_rows()
+
+    for r in range(8):
+        for e in range(2):
+            late_out[r, 4 + e : 5 + e, :] = targets_ref[r + 8 * e : r + 8 * e + 1, :].astype(F32)
+        late_out[r, 6:8, :] = jnp.zeros((2, 256), F32)
+
+    def stem_tile(q):
+        at = GROUP + (16 * (q - 1) if 1 <= q <= 14 else 224 + (q // 15) * 16)
+        return pooled1[at : at + 16, :]
+
+    outer = pooled1[GROUP + 256 : GROUP + 264, :]
+    before = jnp.where(first, 0.0, outer[0:2])
+    after = jnp.where(last, 0.0, outer[2:4])
+    for q in range(16):
+        taps[16 * (q + 2) : 16 * (q + 3), :] = stem_tile(q).astype(BF16)
+    for e in range(2):
+        taps[16 * e : 16 * e + 16, :] = jnp.concatenate(
+            [before[e : e + 1], stem_tile(14 + e)[0:15]], axis=0
+        ).astype(BF16)
+        taps[16 * (18 + e) : 16 * (19 + e), :] = jnp.concatenate(
+            [stem_tile(e)[1:16], after[e : e + 1]], axis=0
+        ).astype(BF16)
 
     def trunk_tile(q):
-        trunk = jnp.dot(lhs[...], conv_w[q], preferred_element_type=F32)
-        trunk = trunk.reshape(LOCAL, 16, 256)
-        block = jnp.maximum(gelu(jnp.max(trunk, axis=1)), gelu(jnp.min(trunk, axis=1)))
+        windows = [taps[16 * k : 16 * k + ROWS, :] for k in range(5)]
+        trunk = jnp.dot(
+            jnp.concatenate(windows, axis=1), conv_w[q], preferred_element_type=F32
+        ).reshape(16, LOCAL, 256)
+        block = jnp.maximum(gelu(jnp.max(trunk, axis=0)), gelu(jnp.min(trunk, axis=0)))
         pooled2[q] = block
         total = jnp.sum(block, axis=0, keepdims=True)
         return total, jnp.sum(block * block, axis=0, keepdims=True)
@@ -290,10 +317,6 @@
     for r in range(8):
         late_out[r, 0:2, :] = stat_all[4:6, :]
         late_out[r, 2:4, :] = stat_all[12:14, :]
-    for r in range(8):
-        for e in range(2):
-            late_out[r, 4 + e : 5 + e, :] = targets_ref[r + 8 * e : r + 8 * e + 1, :].astype(F32)
-        late_out[r, 6:8, :] = jnp.zeros((2, 256), F32)
     send_all(1, lambda peer: late_out.at[peer // 2], late_in)
     late_in[pl.ds(me, 1)] = late_out[pl.ds(rho, 1)]
 
@@ -342,16 +365,15 @@
         ],
         axis=1,
     )
-    emb = jnp.dot(normed, proj[...], preferred_element_type=F32).astype(BF16).astype(F32)
+    emb = jnp.dot(normed, proj[...], preferred_element_type=F32)
     rows_emb = emb[:, 0:CH]
     cols_emb = emb[:, CH : 2 * CH]
+    zero_six = jnp.zeros((6, CH), F32)
     for h in range(2):
-        block = jnp.concatenate([cols_emb[4 * h : 4 * h + 4], cols_emb[8 + 4 * h : 12 + 4 * h]], 0)
+        block = [cols_emb[4 * h : 4 * h + 4], cols_emb[8 + 4 * h : 12 + 4 * h]]
         for r in range(8):
-            emb_out[2 * r + h, 0:8, :] = block
-            emb_out[2 * r + h, 8:9, :] = rows_emb[r : r + 1]
-            emb_out[2 * r + h, 9:10, :] = rows_emb[r + 8 : r + 9]
-            emb_out[2 * r + h, 10:16, :] = jnp.zeros((6, CH), F32)
+            pair = [rows_emb[r : r + 1], rows_emb[r + 8 : r + 9]]
+            emb_out[2 * r + h] = jnp.concatenate(block + pair + [zero_six], 0).astype(BF16)
     send_all(2, lambda peer: emb_out.at[peer], emb_in)
     emb_in[pl.ds(me, 1)] = emb_out[pl.ds(me, 1)]
 
@@ -372,9 +394,10 @@
 
     wait_recv(2, emb_in)
 
+    embs = [emb_in[d].astype(F32) for d in range(N_SEQ)]
     for d in range(N_SEQ):
-        rows_scr[2 * d : 2 * d + 2, :] = emb_in[d, 8:10, :]
-    cols = chain_order(lambda m: emb_in[m // 2, 4 * (m % 2) : 4 * (m % 2) + 4, :])
+        rows_scr[2 * d : 2 * d + 2, :] = embs[d][8:10]
+    cols = chain_order(lambda m: embs[m // 2][4 * (m % 2) : 4 * (m % 2) + 4])
     zero_four = jnp.zeros((4, CH), F32)
 
     def put_row(ref, index, values):
@@ -534,12 +557,13 @@
             pltpu.VMEM((LOCAL, BINS), jnp.int32),
             pltpu.VMEM((2, 8, POOL), jnp.int32),
             pltpu.VMEM((ROWS + 16, POOL), jnp.int32),
+            pltpu.VMEM((ROWS, POOL), jnp.int32),
             pltpu.VMEM((264, POOL), jnp.int32),
             pltpu.VMEM((32, STEM_CH), F32),
             pltpu.VMEM((2, GROUP * POOL, 32), BF16),
             pltpu.VMEM((2, GROUP, STEM_CH), F32),
-            pltpu.VMEM((OFF + ROWS + 16, STEM_CH), F32),
-            pltpu.VMEM((ROWS, 5 * STEM_CH), BF16),
+            pltpu.VMEM((12 * GROUP, STEM_CH), F32),
+            pltpu.VMEM((20 * 16, STEM_CH), BF16),
             pltpu.VMEM((TILES, 5 * STEM_CH, 256), BF16),
             pltpu.VMEM((TILES, LOCAL, 256), F32),
             pltpu.VMEM((TRUNK_CH, 2 * CH), BF16),
@@ -549,8 +573,8 @@
             pltpu.VMEM((N_SEQ, 8, 256), F32),
             pltpu.VMEM((8, 8, 256), F32),
             pltpu.VMEM((N_SEQ, 8, 256), F32),
-            pltpu.VMEM((N_SEQ, 16, CH), F32),
-            pltpu.VMEM((N_SEQ, 16, CH), F32),
+            pltpu.VMEM((N_SEQ, 16, CH), BF16),
+            pltpu.VMEM((N_SEQ, 16, CH), BF16),
             pltpu.VMEM((CH, BINS), F32),
             pltpu.VMEM((BINS, CH), F32),
             pltpu.VMEM((12 * CH, 2 * CH), BF16),

time: 47.8 us -> 46.9 us (0.981)
  Pallas kernels: 46.9 us -> 46.1 us
    pallas_call x1, Pallas kernels: 45.4 us -> 44.5 us  [per_device(): pl.pallas_call(fused, out_shape=shapes, in_specs=[hbm] * 8, out_specs=(vm...]
where the time goes in v4:
time: 46.9 us; the launch traced here: 46.7 us
  Pallas kernels  46.1 us (98%)
  between operations  0.64 us (1%)
    pallas_call x1, Pallas kernels, per_device(): pl.pallas_call(fused, out_shape=shapes, in_specs=[hbm] * 8, out_specs=(vm...  44.5 us
    pallas_call x1, Pallas kernels, per_device(): pl.pallas_call(deliver, out_shape=shapes, in_specs=[vmem, vmem], out_spec...  1.56 us

profile of v4, /device:TPU:1, one launch (start us, length us, event | category | flops | bytes accessed | tf_op | source)
XLA Modules:
  0.0 46.7 jit_solution(7601225511819478976)
XLA Ops:
  0.6 44.5 %shard_map.95 = (f32[16,256]{1,0:T(8,128)}, f32[16,1536]{1,0:T(8,128)}) custom-call(s32[256,128]{1,0:T(8,128)} %bitcast.6, bf16[20,768]{1,0:T(8,128)(2,1)} %stem_hbm.1, bf16[3840,1536]{1,0:T(8,128)(2,1)} %bitcast.4, bf16[1536,128]{1,0:T(8,128)(2,1)} %row_proj_ref.1, bf16[1536,128]{1,0:T(8,128)(2,1)} %col_proj_ref.1, bf16[1152,128]{1,0:T(8,128)(2,1)} %bitcast.5, ...), custom_call_target="tpu_custom_call" | custom-call | tf_op jit(solution)/shard_map/pallas_call | solution.py:548
  45.2 1.6 %shard_map.96 = (f32[16,256]{1,0:T(8,128)}, f32[16,1536]{1,0:T(8,128)}) custom-call(f32[16,256]{1,0:T(8,128)} %get-tuple-element.4.pred_in, f32[16,1536]{1,0:T(8,128)} %get-tuple-element.5.grad_in), custom_call_target="tpu_custom_call" | custom-call | tf_op jit(solution)/shard_map/pallas_call | solution.py:612

commit v5 on v4

--- a/solution.py
+++ b/solution.py
@@ -323,27 +323,15 @@
     for copy in weight_copies:
         copy.wait()
     zero_block = jnp.zeros((CH, CH), BF16)
-    for a in range(4):
+
+    def place_weights(ref, block):
         for b in range(3):
-            at = (3 * a + b) * CH
-            near = pair_ref[(3 * a + b) * CH : (3 * a + b + 1) * CH, :] if a < 3 else zero_block
-            far = (
-                pair_ref[(3 * (a - 1) + b) * CH : (3 * (a - 1) + b + 1) * CH, :]
-                if a > 0
-                else zero_block
-            )
-            fwd_w[at : at + CH, :] = jnp.concatenate([near, far], axis=1)
-            near = (
-                pair_ref[(3 * (2 - a) + 2 - b) * CH : (3 * (2 - a) + 3 - b) * CH, :].T
-                if a < 3
-                else zero_block
-            )
-            far = (
-                pair_ref[(3 * (3 - a) + 2 - b) * CH : (3 * (3 - a) + 3 - b) * CH, :].T
-                if a > 0
-                else zero_block
-            )
-            bwd_w[at : at + CH, :] = jnp.concatenate([near, far], axis=1)
+            blocks = [zero_block] + [block(a, b) for a in range(3)] + [zero_block]
+            for a in range(4):
+                at = (3 * a + b) * CH
+                ref[at : at + CH, :] = jnp.concatenate([blocks[a + 1], blocks[a]], axis=1)
+
+    place_weights(fwd_w, lambda a, b: pair_ref[(3 * a + b) * CH : (3 * a + b + 1) * CH, :])
 
     zero_row = jnp.zeros((160, CH), BF16)
     hid[0] = zero_row
@@ -377,6 +365,9 @@
     send_all(2, lambda peer: emb_out.at[peer], emb_in)
     emb_in[pl.ds(me, 1)] = emb_out[pl.ds(me, 1)]
 
+    place_weights(
+        bwd_w, lambda a, b: pair_ref[(8 - 3 * a - b) * CH : (9 - 3 * a - b) * CH, :].T
+    )
     tgt_rows[...] = jnp.zeros_like(tgt_rows)
     for d in range(N_SEQ):
         tgt_rows[2 * d : 2 * d + 2, :] = late_in[d, 4:6, :]

time: 46.9 us -> 46.9 us (level)
  no operation moved by 1% of the time
where the time goes in v5:
time: 46.9 us; the launch traced here: 46.7 us
  Pallas kernels  46.1 us (98%)
  between operations  0.64 us (1%)
    pallas_call x1, Pallas kernels, per_device(): pl.pallas_call(fused, out_shape=shapes, in_specs=[hbm] * 8, out_specs=(vm...  44.5 us
    pallas_call x1, Pallas kernels, per_device(): pl.pallas_call(deliver, out_shape=shapes, in_specs=[vmem, vmem], out_spec...  1.56 us

profile of v5, /device:TPU:1, one launch (start us, length us, event | category | flops | bytes accessed | tf_op | source)
XLA Modules:
  0.0 46.7 jit_solution(5086673638924449268)
XLA Ops:
  0.6 44.5 %shard_map.95 = (f32[16,256]{1,0:T(8,128)}, f32[16,1536]{1,0:T(8,128)}) custom-call(s32[256,128]{1,0:T(8,128)} %bitcast.6, bf16[20,768]{1,0:T(8,128)(2,1)} %stem_hbm.1, bf16[3840,1536]{1,0:T(8,128)(2,1)} %bitcast.4, bf16[1536,128]{1,0:T(8,128)(2,1)} %row_proj_ref.1, bf16[1536,128]{1,0:T(8,128)(2,1)} %col_proj_ref.1, bf16[1152,128]{1,0:T(8,128)(2,1)} %bitcast.5, ...), custom_call_target="tpu_custom_call" | custom-call | tf_op jit(solution)/shard_map/pallas_call | solution.py:539
  45.2 1.6 %shard_map.96 = (f32[16,256]{1,0:T(8,128)}, f32[16,1536]{1,0:T(8,128)}) custom-call(f32[16,256]{1,0:T(8,128)} %get-tuple-element.4.pred_in, f32[16,1536]{1,0:T(8,128)} %get-tuple-element.5.grad_in), custom_call_target="tpu_custom_call" | custom-call | tf_op jit(solution)/shard_map/pallas_call | solution.py:603

commit v6 on v5

--- a/solution.py
+++ b/solution.py
@@ -180,7 +180,7 @@
             total = total + (before << (3 * (2 - shift))) + (after << (3 * (2 + shift)))
         return total
 
-    codes_in_order[...] = code_rows(8, ROWS)
+    codes_in_order[0:ROWS, :] = code_rows(8, ROWS)
     for q in range(1, 15):
         codes[16 * (q - 1) : 16 * q, :] = codes_in_order[pl.ds(q, 16, stride=16), :]
 
@@ -548,7 +548,7 @@
             pltpu.VMEM((LOCAL, BINS), jnp.int32),
             pltpu.VMEM((2, 8, POOL), jnp.int32),
             pltpu.VMEM((ROWS + 16, POOL), jnp.int32),
-            pltpu.VMEM((ROWS, POOL), jnp.int32),
+            pltpu.VMEM((ROWS + 16, POOL), jnp.int32),
             pltpu.VMEM((264, POOL), jnp.int32),
             pltpu.VMEM((32, STEM_CH), F32),
             pltpu.VMEM((2, GROUP * POOL, 32), BF16),

time: 46.9 us -> 46.8 us (level)
  no operation moved by 1% of the time
where the time goes in v6:
time: 46.8 us; the launch traced here: 46.6 us
  Pallas kernels  46 us (98%)
  between operations  0.64 us (1%)
    pallas_call x1, Pallas kernels, per_device(): pl.pallas_call(fused, out_shape=shapes, in_specs=[hbm] * 8, out_specs=(vm...  44.4 us
    pallas_call x1, Pallas kernels, per_device(): pl.pallas_call(deliver, out_shape=shapes, in_specs=[vmem, vmem], out_spec...  1.56 us

profile of v6, /device:TPU:1, one launch (start us, length us, event | category | flops | bytes accessed | tf_op | source)
XLA Modules:
  0.0 46.6 jit_solution(9423092443402540181)
XLA Ops:
  0.6 44.4 %shard_map.95 = (f32[16,256]{1,0:T(8,128)}, f32[16,1536]{1,0:T(8,128)}) custom-call(s32[256,128]{1,0:T(8,128)} %bitcast.6, bf16[20,768]{1,0:T(8,128)(2,1)} %stem_hbm.1, bf16[3840,1536]{1,0:T(8,128)(2,1)} %bitcast.4, bf16[1536,128]{1,0:T(8,128)(2,1)} %row_proj_ref.1, bf16[1536,128]{1,0:T(8,128)(2,1)} %col_proj_ref.1, bf16[1152,128]{1,0:T(8,128)(2,1)} %bitcast.5, ...), custom_call_target="tpu_custom_call" | custom-call | tf_op jit(solution)/shard_map/pallas_call | solution.py:539
  45.1 1.6 %shard_map.96 = (f32[16,256]{1,0:T(8,128)}, f32[16,1536]{1,0:T(8,128)}) custom-call(f32[16,256]{1,0:T(8,128)} %get-tuple-element.4.pred_in, f32[16,1536]{1,0:T(8,128)} %get-tuple-element.5.grad_in), custom_call_target="tpu_custom_call" | custom-call | tf_op jit(solution)/shard_map/pallas_call | solution.py:603
